TPU v7x, 32 devices: a whole 2x2x4 slice. The times are simulated.
32 devices in a mesh: dp: 4 (over y, x), seq: 4 (over z), head: 2 (over core).
Axes of the slice: x: 2, y: 2, z: 4, core: 2. Of those that a mesh axis runs over, the one named last changes fastest.
Arguments:
- states: bfloat16 [4, 512, 2432], P('dp', 'seq'), may hold values from -6 to 6
- adjoint: float32 [4, 512, 2432], P('dp', 'seq'), may hold values from -16 to 16
- text_kv: bfloat16 [4, 32, 2, 1280], P('dp', 'seq', None, 'head'), may hold values from -125 to 125
- text_len: int32 [4], P('dp'), may hold values from 8 to 32, as said below
- step_index: int32 [4], P('dp'), may hold values from 0 to 27
- modulation: float32 [28, 3, 2432], replicated, may hold values from -3 to 3
- w_qkv: bfloat16 [2432, 3, 1280], P('dp', None, 'head'), may hold values from -0.125 to 0.125
- qk_gain: float32 [2, 64], replicated, may hold values from 0.1 to 1.9
- w_out: bfloat16 [1280, 2432], P('head', 'dp'), may hold values from -0.15625 to 0.15625
Outputs:
- pulled: float32 [4, 512, 2432], P('dp', 'seq', 'head')
Inputs may be any that keep to these rules, and one draw needn't show every extreme that they name: `text_len`: some trajectory has all 32 text tokens and some has 8.
All inputs are finite; a program needn't handle non-finite values.
Results may differ from a plain program's by a relative error of at most 0.02.
The roundings to bfloat16 on the way count: a program that leaves them out, or rounds other values in their place, can miss the bound.
Values may be sent and summed in bfloat16 or wider, within the bound.
No kernel may reach another device: no remote copies, remote signals or barrier semaphores. Data moves between devices by JAX's collectives and lax.ppermute only.
A program may use at most 192 MiB of HBM per device.

v0:
```python
import functools

import jax
import jax.numpy as jnp
from jax import lax
from jax.experimental import pallas as pl
from jax.experimental.pallas import tpu as pltpu
from jax.sharding import PartitionSpec as P

HD = 64
GRANT = 60 * 1024 * 1024
SMALL_GRANT = 24 * 1024 * 1024
EXTRA = 128
NT = (((1,), (1,)), ((), ()))
NN = (((1,), (0,)), ((), ()))


def line_ring(count):
    return [0] + list(range(1, count, 2)) + [i for i in range(count - 1, 0, -1) if i % 2 == 0]


def ring_pairs(order):
    return [(order[i], order[(i + 1) % len(order)]) for i in range(len(order))]


def ring_place(order, index):
    place = jnp.int32(0)
    for position, member in enumerate(order):
        place = jnp.where(index == member, jnp.int32(position), place)
    return place


def ring_member(order, place):
    member = jnp.int32(order[0])
    for position, value in enumerate(order):
        member = jnp.where(place == position, jnp.int32(value), member)
    return member


def dot(a, b, dims):
    return lax.dot_general(a, b, dims, preferred_element_type=jnp.float32)


def equal_blocks(columns, block):
    row = lax.broadcasted_iota(jnp.int32, (columns, columns), 0)
    column = lax.broadcasted_iota(jnp.int32, (columns, columns), 1)
    return jnp.where(row // block == column // block, 1.0, 0.0).astype(jnp.bfloat16)


def head_means(values):
    ones = equal_blocks(values.shape[1], HD)
    total = 0.0
    for n in range(3):
        term = values.astype(jnp.bfloat16)
        total = total + dot(term, ones, NN)
        if n < 2:
            values = values - term.astype(jnp.float32)
    return total * (1.0 / HD)


def head_gains(gain, slots):
    return jnp.concatenate([gain[0:1, :]] * slots + [gain[1:2, :]] * slots, axis=1)


def whole_tiles(columns):
    return -(-columns // 128) * 128


def spec(space):
    return pl.BlockSpec(memory_space=space)


def text_columns(text, part):
    rows = text[...].astype(jnp.float32)[:, part, :]
    return [rows[:, c * EXTRA : (c + 1) * EXTRA] for c in range(rows.shape[1] // EXTRA)]


def extra_columns(blocks, rows):
    filled = sum(one.shape[0] for one in blocks)
    blocks = blocks + [jnp.zeros((rows - filled, EXTRA), jnp.float32)]
    return jnp.concatenate(blocks, axis=0).astype(jnp.bfloat16)


def first_kernel(step, core, states, table, adjoint, text, out, rows_out, extra_out):
    rows = [table[c, pl.ds(step[0], 1), :] for c in range(3)]
    widened = states[...].astype(jnp.float32)
    centered = widened - jnp.mean(widened, axis=-1, keepdims=True)
    inv_std = lax.rsqrt(jnp.mean(centered * centered, axis=-1, keepdims=True) + 1e-06)
    half, width = states.shape
    out[:, :width] = (centered * inv_std * (1.0 + rows[1]) + rows[0]).astype(jnp.bfloat16)
    for c in range(3):
        rows_out[c : c + 1, :] = rows[c]
    squares = jnp.sum(adjoint[...] * adjoint[...], axis=0, keepdims=True)
    squares = jnp.sum(squares, axis=1, keepdims=True)
    terms = []
    for n in range(3):
        terms.append(squares.astype(jnp.bfloat16).astype(jnp.float32))
        squares = squares - terms[-1]
    lane = lax.broadcasted_iota(jnp.int32, (8, EXTRA), 1)
    sums = jnp.where(lane == 0, terms[0], jnp.where(lane == 1, terms[1], jnp.where(lane == 2, terms[2], 0.0)))
    extra = extra_columns(text_columns(text, 0) + [sums], half)
    out[:, width:] = extra
    extra_out[...] = extra


def first_call(step, core, states, table, adjoint, text):
    rows, width = states.shape
    half = rows // 2
    whole = lambda *shape: pl.BlockSpec(shape, lambda i, step, core: (0,) * len(shape))
    return pl.pallas_call(
        first_kernel,
        out_shape=(
            jax.ShapeDtypeStruct((half, width + EXTRA), jnp.bfloat16),
            jax.ShapeDtypeStruct((8, width), jnp.float32),
            jax.ShapeDtypeStruct((half, EXTRA), jnp.bfloat16),
        ),
        grid_spec=pltpu.PrefetchScalarGridSpec(
            num_scalar_prefetch=2,
            grid=(1,),
            in_specs=[
                pl.BlockSpec((half, width), lambda i, step, core: (core[0], 0)),
                whole(*table.shape),
                whole(*adjoint.shape),
                whole(*text.shape),
            ],
            out_specs=(whole(half, width + EXTRA), whole(8, width), whole(half, EXTRA)),
        ),
        compiler_params=pltpu.CompilerParams(vmem_limit_bytes=GRANT),
        cost_estimate=pl.CostEstimate(flops=8 * half * width, bytes_accessed=16 * half * width, transcendentals=0),
    )(step, core, states, table, adjoint, text)


def pick_half(core, rows):
    half = rows.shape[1] // 2
    return jnp.where(core == 0, rows[:, :half], rows[:, half:])


def modulate_kernel(core, states, table_rows, extra, out, normed_out, stretch_out, inv_out):
    widened = states[...].astype(jnp.float32)
    centered = widened - jnp.mean(widened, axis=-1, keepdims=True)
    inv_std = lax.rsqrt(jnp.mean(centered * centered, axis=-1, keepdims=True) + 1e-06)
    normed = centered * inv_std
    scale = 1.0 + table_rows[1:2, :]
    rows, width = states.shape
    out[:, :width] = (normed * scale + table_rows[0:1, :]).astype(jnp.bfloat16)
    for n in range(2):
        out[n * rows // 2 : (n + 1) * rows // 2, width:] = extra[...]
    normed_out[...] = pick_half(core[0], normed)
    stretch_out[...] = pick_half(core[0], scale)
    inv_out[...] = jnp.broadcast_to(inv_std, inv_out.shape)


def cotangent_kernel(limit, core, adjoint, table_rows, text, extra, previous, following, opposite, out, half_out, base_out):
    quarter = opposite.shape[0]
    first = 2 * quarter - opposite.shape[0]
    row = 8 * (text.shape[2] // EXTRA)
    squares = None
    for terms in (extra[...], previous[...], following[...]):
        terms = terms.astype(jnp.float32)[row : row + 1, :]
        squares = terms if squares is None else squares + terms
    squares = squares + opposite[...].astype(jnp.float32)[row - first : row - first + 1, :]
    squares = jnp.sum(squares, axis=1, keepdims=True)
    clip_scale = jnp.minimum(1.0, limit / jnp.sqrt(squares + 1e-06))
    gating = table_rows[2:3, :]
    clipped = clip_scale * adjoint[...]
    rows, width = adjoint.shape
    half = rows // 2
    columns = extra_columns(text_columns(text, 1), half)
    out[:, :width] = (gating * clipped).astype(jnp.bfloat16)
    for n in range(2):
        out[n * half : (n + 1) * half, width:] = columns
    base_out[...] = pick_half(core[0], clipped)
    own = adjoint[pl.ds(pl.multiple_of(core[0] * half, 8), half), :]
    half_out[:, :width] = (gating * (clip_scale * own)).astype(jnp.bfloat16)
    half_out[:, width:] = columns


def cotangent_call(limit, core, adjoint, table_rows, text, extra, previous, following, opposite):
    rows, width = adjoint.shape
    bf16 = jnp.bfloat16
    block = width // EXTRA
    whole = lambda one: pl.BlockSpec(one.shape, lambda i, core: (0,) * one.ndim)
    tail = lambda one: pl.BlockSpec((one.shape[0], EXTRA), lambda i, core: (0, block))
    outs = (
        jax.ShapeDtypeStruct((rows, width + EXTRA), bf16),
        jax.ShapeDtypeStruct((rows // 2, width + EXTRA), bf16),
        jax.ShapeDtypeStruct((rows, width // 2), jnp.float32),
    )
    return pl.pallas_call(
        functools.partial(cotangent_kernel, limit),
        out_shape=outs,
        grid_spec=pltpu.PrefetchScalarGridSpec(
            num_scalar_prefetch=1,
            grid=(1,),
            in_specs=[whole(adjoint), whole(table_rows), whole(text), whole(extra)]
            + [tail(one) for one in (previous, following, opposite)],
            out_specs=tuple(whole(one) for one in outs),
        ),
        compiler_params=pltpu.CompilerParams(vmem_limit_bytes=SMALL_GRANT),
        cost_estimate=pl.CostEstimate(flops=4 * rows * width, bytes_accessed=12 * rows * width, transcendentals=0),
    )(core, adjoint, table_rows, text, extra, previous, following, opposite)


class Copies:
    def __init__(self, sems):
        self.sems = sems
        self.count = 0

    def start(self, source, target):
        copy = pltpu.make_async_copy(source, target, self.sems.at[self.count])
        copy.start()
        self.count += 1
        return copy

    def weights(self, scalars, w_in, w_all, shard, first=0):
        columns = w_in[0].shape[1] - first
        return [
            self.start(
                piece.at[:, pl.ds(first, columns)],
                w_all.at[
                    pl.ds(pl.multiple_of(scalars[1 + n % 4] * shard, 16), shard),
                    pl.ds(n // 4 * columns, columns),
                ],
            )
            for n, piece in enumerate(w_in)
        ]

    def rows(self, core, pieces, target, rows):
        half = rows // 2
        copies = [self.start(pieces[0], target.at[pl.ds(0, rows)])]
        places = [(rows, half), (3 * rows, half)]
        parts = (len(pieces) - 5) // 2
        places += [(2 * rows + n * half // parts, half // parts) for n in range(parts)]
        for n, (first, size) in enumerate(places):
            for m, holder in enumerate((core, 1 - core)):
                there = pl.ds(pl.multiple_of(first + holder * half, 16), size)
                copies.append(self.start(pieces[1 + 2 * n + m], target.at[there]))
        return copies


def window_heads(scalars, count, rows, text_dev, gathered, width, extra, text, text_t=None):
    half = rows // 2
    for k in range(count):
        there = pl.ds(pl.multiple_of(k * rows + scalars[0] * half, 16), half)
        extra[k] = gathered[there, width:].astype(jnp.float32)
    for i in range(text.shape[0]):
        head = scalars[5] + i
        first = pl.ds(pl.multiple_of(head // 2 * text_dev, 8), text_dev)
        found = jnp.concatenate([extra[k, first, :] for k in range(count)], axis=0)
        found = jnp.where(head % 2 == 0, found[:, :HD], found[:, HD:])
        text[i] = found.astype(jnp.bfloat16)
        if text_t is not None:
            text_t[i] = found.T.astype(jnp.bfloat16)


def project_kernel(slots, count, rows, shard, width, text_dev, scalars, gain, *refs):
    refs = list(refs)
    take = lambda n: [refs.pop(0) for _ in range(n)]
    mod_in = take(9)
    w_in = take(8)
    qkv, k_t, raw_all, inv_all, text, text_t, w_keep, w_give = take(8)
    w_all, mod_all, sems, extra = take(4)
    inner = slots * HD
    core = scalars[0]
    copies = Copies(sems)
    w_copies = copies.weights(scalars, w_in, w_all, shard)
    row_copies = copies.rows(core, mod_in, mod_all, rows)

    lane = lax.broadcasted_iota(jnp.int32, (1, 2 * inner), 1)
    gains = head_gains(gain, slots) * jnp.where(lane < inner, HD ** (-0.5), 1.0)
    identity = equal_blocks(inner, 1)
    for copy in w_copies:
        copy.wait()
    half = width // 2
    columns = pl.ds(0, w_keep.shape[1])
    half_copies = [
        copies.start(w_all.at[pl.ds(pl.multiple_of(holder * half, 16), half), columns], target)
        for holder, target in ((core, w_keep), (1 - core, w_give))
    ]
    for copy in row_copies:
        copy.wait()
    window_heads(scalars, count, rows, text_dev, mod_all, width, extra, text, text_t)
    span = 2 * rows
    for b in range(count // 2):
        here = slice(b * span, (b + 1) * span)
        projected = jnp.dot(
            mod_all[here, :width], w_all[:, : 3 * inner], preferred_element_type=jnp.float32
        )
        raw = projected[:, : 2 * inner]
        inverse = lax.rsqrt(head_means(raw * raw) + 1e-06)
        raw_all[here, :] = raw
        inv_all[here, :] = inverse
        qkv[here, : 2 * inner] = (raw * inverse * gains).astype(jnp.bfloat16)
        qkv[here, 2 * inner :] = projected[:, 2 * inner :].astype(jnp.bfloat16)
        k_t[:, here] = dot(identity, qkv[here, inner : 2 * inner], NT).astype(jnp.bfloat16)
    for copy in half_copies:
        copy.wait()


def attend_kernel(slots, count, rows, shard, width, text_dev, first_column, scalars, gain, *refs):
    refs = list(refs)
    take = lambda n: [refs.pop(0) for _ in range(n)]
    projected = take(8)
    cot_in = take(7)
    w_in = take(4)
    mine_out, theirs_out, rest_out = take(3)
    w_out, cot_all, sems, extra, values_text = take(5)
    d_all, grads, stacked = take(3)
    qkv, k_t, raw_all, inv_all, text, text_t, w_keep, w_give = refs
    inner = slots * HD
    tokens = rows * count
    core = scalars[0]
    copies = Copies(sems)
    w_copies = copies.weights(scalars, w_in, w_out, shard, first_column)
    row_copies = copies.rows(core, cot_in, cot_all, rows)
    local_copies = [copies.start(*one) for one in zip(projected, refs)]
    score_scale = HD ** (-0.5)
    span = 2 * rows

    text_rows = count * text_dev
    row = lax.broadcasted_iota(jnp.int32, (text_rows, span), 0)
    text_id = row
    for k in range(count):
        inside = (row >= k * text_dev) & (row < (k + 1) * text_dev)
        text_id = jnp.where(inside, row + (scalars[7 + k] - k) * text_dev, text_id)
    bias = jnp.where(text_id < scalars[6], 0.0, -1e30)

    for copy in w_copies:
        copy.wait()
    arrivals = [row_copies[:3], row_copies[3:]]
    for b in range(count // 2):
        for copy in arrivals[b]:
            copy.wait()
        here = slice(b * span, (b + 1) * span)
        out_grad = jnp.dot(cot_all[here, :width], w_out[...], preferred_element_type=jnp.float32)
        d_all[here, :] = out_grad.astype(jnp.bfloat16)
    window_heads(scalars, count, rows, text_dev, cot_all, width, extra, values_text)
    for copy in local_copies[:6]:
        copy.wait()

    d_first = d_all.shape[1] - inner
    for i in range(slots):
        columns = [slice(n * inner + i * HD, n * inner + (i + 1) * HD) for n in range(3)]
        keys, values = qkv[:, columns[1]], qkv[:, columns[2]]
        keys_t = k_t[i * HD : (i + 1) * HD, :]
        grad_k, grad_v = 0.0, 0.0
        for b in range(count // 2):
            here = slice(b * span, (b + 1) * span)
            query = qkv[here, columns[0]]
            grad = d_all[here, d_first + i * HD : d_first + (i + 1) * HD]
            scores = dot(keys, query, NT)
            text_scores = dot(text[i], query, NT) + bias
            col_max = jnp.maximum(
                jnp.max(scores, axis=0, keepdims=True), jnp.max(text_scores, axis=0, keepdims=True)
            )
            exps = jnp.exp(scores - col_max)
            text_exps = jnp.exp(text_scores - col_max)
            total = jnp.sum(exps, axis=0, keepdims=True) + jnp.sum(text_exps, axis=0, keepdims=True)
            inverse = 1.0 / total
            grad_w = dot(values, grad, NT)
            text_grad_w = dot(values_text[i], grad, NT)
            delta = inverse * (
                jnp.sum(exps * grad_w, axis=0, keepdims=True)
                + jnp.sum(text_exps * text_grad_w, axis=0, keepdims=True)
            )
            weights = exps * inverse
            grad_s = (weights * (grad_w - delta)).astype(jnp.bfloat16)
            text_grad_s = (text_exps * inverse * (text_grad_w - delta)).astype(jnp.bfloat16)
            grad_k += dot(grad_s, query, NN)
            grad_v += dot(weights.astype(jnp.bfloat16), grad, NN)
            grad_q = dot(keys_t, grad_s, NN) + dot(text_t[i], text_grad_s, NN)
            grads[here, columns[0]] = grad_q.T * score_scale
        grads[:, columns[1]] = grad_k
        grads[:, columns[2]] = grad_v

    lane = lax.broadcasted_iota(jnp.int32, (1, inner), 1)
    mine = jnp.zeros((1, inner), jnp.float32)
    for i in range(slots):
        inside = (lane >= i * HD) & (lane < (i + 1) * HD) & (scalars[7 + count + i] > 0)
        mine = jnp.where(inside, 1.0, mine)
    gains = head_gains(gain, slots)
    for b in range(count // 2):
        here = slice(b * span, (b + 1) * span)
        scaled = grads[here, : 2 * inner].astype(jnp.bfloat16).astype(jnp.float32) * gains
        raw, inverse = raw_all[here, :], inv_all[here, :]
        back = scaled * inverse - raw * head_means(scaled * raw) * (inverse * inverse * inverse)
        valid = jnp.concatenate([mine, mine], axis=1) > 0.0
        stacked[here, : 2 * inner] = jnp.where(valid, back, 0.0).astype(jnp.bfloat16)
        back = jnp.where(mine > 0.0, grads[here, 2 * inner :], 0.0).astype(jnp.bfloat16)
        stacked[here, 2 * inner : 3 * inner] = back
    stacked[:, 3 * inner :] = jnp.zeros((tokens, stacked.shape[1] - 3 * inner), jnp.bfloat16)
    first = stacked[rows : 2 * rows, :]
    rest_out[: (count - 2) * rows, :] = stacked[2 * rows :, :]
    rest_out[(count - 2) * rows :, :] = stacked[:rows, :]
    for copy in local_copies[6:]:
        copy.wait()
    theirs_out[...] = dot(first, w_give[...], NT).astype(jnp.bfloat16)
    mine_out[...] = dot(first, w_keep[...], NT)


def project_call(scalars, gain, mod, weights, slots, rows, text_dev, count):
    shard = weights[0].shape[0]
    columns = 4 * slots * HD
    width = mod[0].shape[1] - EXTRA
    tokens = rows * count
    text_rows = text_dev * count
    f32, bf16 = jnp.float32, jnp.bfloat16
    vmem, hbm = spec(pltpu.VMEM), spec(pl.ANY)
    inner = slots * HD
    shapes = [((tokens, 3 * inner), bf16), ((inner, tokens), bf16)] + [((tokens, 2 * inner), f32)] * 2
    shapes += [((slots, text_rows, HD), bf16), ((slots, HD, text_rows), bf16)]
    shapes += [((width // 2, whole_tiles(3 * slots * HD)), bf16)] * 2
    return pl.pallas_call(
        functools.partial(project_kernel, slots, count, rows, shard, width, text_dev),
        out_shape=tuple(jax.ShapeDtypeStruct(*one) for one in shapes),
        in_specs=[spec(pltpu.SMEM), vmem] + [hbm] * (len(mod) + len(weights)),
        out_specs=(vmem,) * (len(shapes) - 2) + (hbm,) * 2,
        scratch_shapes=[
            pltpu.VMEM((width, columns), bf16),
            pltpu.VMEM((tokens, width + EXTRA), bf16),
            pltpu.SemaphoreType.DMA((len(mod) + len(weights) + 2,)),
            pltpu.VMEM((count, rows // 2, EXTRA), f32),
        ],
        compiler_params=pltpu.CompilerParams(vmem_limit_bytes=GRANT),
        cost_estimate=pl.CostEstimate(
            flops=2 * tokens * width * 3 * slots * HD,
            bytes_accessed=2 * (tokens * width + columns * width) + 4 * tokens * columns,
            transcendentals=0,
        ),
    )(scalars, gain, *mod, *weights)


def attend_call(scalars, gain, operands, cot, weights, slots, rows, text_dev):
    count = operands[0].shape[0] // rows
    shard, columns = weights[0].shape
    width = cot[0].shape[1] - EXTRA
    tokens = rows * count
    inner = slots * HD
    stacked = whole_tiles(3 * inner)
    first = (columns - inner) // 128 * 128
    f32, bf16 = jnp.float32, jnp.bfloat16
    vmem, hbm = spec(pltpu.VMEM), spec(pl.ANY)
    shapes = [((rows, width // 2), f32), ((rows, width // 2), bf16), ((tokens - rows, stacked), bf16)]
    return pl.pallas_call(
        functools.partial(attend_kernel, slots, count, rows, shard, width, text_dev, first),
        out_shape=tuple(jax.ShapeDtypeStruct(*one) for one in shapes),
        in_specs=[spec(pltpu.SMEM), vmem] + [hbm] * (len(operands) + len(cot) + len(weights)),
        out_specs=(vmem,) * len(shapes),
        scratch_shapes=[
            pltpu.VMEM((width, columns - first), bf16),
            pltpu.VMEM((tokens, width + EXTRA), bf16),
            pltpu.SemaphoreType.DMA((len(operands) + len(cot) + len(weights),)),
            pltpu.VMEM((count, rows // 2, EXTRA), f32),
            pltpu.VMEM((slots, text_dev * count, HD), bf16),
            pltpu.VMEM((tokens, columns - first), bf16),
            pltpu.VMEM((tokens, 3 * inner), f32),
            pltpu.VMEM((tokens, stacked), bf16),
        ]
        + [pltpu.VMEM(one.shape, one.dtype) for one in operands],
        compiler_params=pltpu.CompilerParams(vmem_limit_bytes=GRANT),
        cost_estimate=pl.CostEstimate(
            flops=2 * tokens * width * inner + 10 * tokens * tokens * inner,
            bytes_accessed=2 * (tokens * width + columns * width),
            transcendentals=slots * tokens * tokens,
        ),
    )(scalars, gain, *operands, *cot, *weights)


def backward_kernel(own, other, w_own, w_other, *outs):
    total = dot(own[...], w_own[...], NT) + dot(other[...], w_other[...], NT)
    part = outs[0].shape[0]
    for n, out in enumerate(outs):
        out[...] = total[n * part : (n + 1) * part].astype(out.dtype)


def backward_call(own, other, w_own, w_other, part, dtype):
    rows, inner = own.shape
    half = w_own.shape[0]
    vmem = spec(pltpu.VMEM)
    return pl.pallas_call(
        backward_kernel,
        out_shape=(jax.ShapeDtypeStruct((part, half), dtype),) * (rows // part),
        in_specs=[vmem] * 4,
        out_specs=(vmem,) * (rows // part),
        compiler_params=pltpu.CompilerParams(vmem_limit_bytes=SMALL_GRANT),
        cost_estimate=pl.CostEstimate(
            flops=4 * rows * half * inner,
            bytes_accessed=4 * (rows + half) * inner + 4 * rows * half,
            transcendentals=0,
        ),
    )(own, other, w_own, w_other)


def sums_kernel(own_near, own_far, near, far, scale, normed, grad_out, sums_out):
    half = near.shape[0]
    for part, (own, moving) in enumerate(((own_near, near), (own_far, far))):
        here = slice(part * half, (part + 1) * half)
        grad = (own[...] + moving[...].astype(jnp.float32)) * scale[...]
        grad_out[here, :] = grad
        first = jnp.sum(grad, axis=-1, keepdims=True)
        second = jnp.sum(grad * normed[here, :], axis=-1, keepdims=True)
        lane = lax.broadcasted_iota(jnp.int32, (half, 128), 1)
        sums_out[here, :] = jnp.where(lane == 0, first, second)


def last_kernel(width, grad, sums, other, normed, base, inv_std, out):
    total = (sums[...] + other[...]) * (1.0 / width)
    rows = base[...] + inv_std[:, 0:1] * (
        grad[...] - total[:, 0:1] - normed[...] * total[:, 1:2]
    )
    out[...] = rows.T


def local_call(kernel, shapes, scalar_count, *operands):
    vmem = spec(pltpu.VMEM)
    return pl.pallas_call(
        kernel,
        out_shape=tuple(jax.ShapeDtypeStruct(*one) for one in shapes),
        in_specs=[spec(pltpu.SMEM)] * scalar_count + [vmem] * (len(operands) - scalar_count),
        out_specs=(vmem,) * len(shapes),
        compiler_params=pltpu.CompilerParams(vmem_limit_bytes=SMALL_GRANT),
        cost_estimate=pl.CostEstimate(
            flops=sum(one.size for one in operands),
            bytes_accessed=sum(one.size * one.dtype.itemsize for one in operands),
            transcendentals=0,
        ),
    )(*operands)


def shards_by_head(states, adjoint, text_kv, text_len, step_index, modulation, w_qkv, qk_gain, w_out):
    hidden_state = states[0]
    adjoint_rows = adjoint[0]
    tok_count, model_width = hidden_state.shape
    seq_count = lax.axis_size("seq")
    inner_dev = w_qkv.shape[2]
    heads_dev = inner_dev // HD
    shard = w_qkv.shape[0]
    slots = -(-heads_dev // seq_count)
    inner = slots * HD
    half_rows = tok_count // 2
    half_width = model_width // 2
    f32, bf16 = jnp.float32, jnp.bfloat16
    core = lax.axis_index("head").astype(jnp.int32)
    seq_index = lax.axis_index("seq")
    dp_index = lax.axis_index("dp")
    pin = lax.optimization_barrier

    seq_order = line_ring(seq_count)
    seq_place = ring_place(seq_order, seq_index)
    seq_next = ring_pairs(seq_order)
    swap = [(0, 1), (1, 0)]
    first_way = [(2 * p + c, 2 * (p ^ (1 + c)) + c) for p in range(4) for c in range(2)]
    second_way = [(2 * p + c, 2 * (p ^ (2 - c)) + c) for p in range(4) for c in range(2)]

    first = seq_index * heads_dev // seq_count
    stop = (seq_index + 1) * heads_dev // seq_count
    window = jnp.minimum(first, heads_dev - slots)
    valid = [(window + i >= first) & (window + i < stop) for i in range(slots)]
    owners = [ring_member(seq_order, (seq_place - k + seq_count) % seq_count) for k in range(seq_count)]
    w_index = [dp_index, dp_index ^ (1 + core), dp_index ^ (2 - core), dp_index ^ 3]
    scalars = [core] + w_index + [window, text_len[0]] + owners + valid
    scalars = jnp.stack([one.astype(jnp.int32) for one in scalars])

    def step(moving):
        return lax.ppermute(moving, "seq", seq_next)

    def other_core(moving):
        return lax.ppermute(moving, "head", swap)

    def step_back(moving):
        return lax.ppermute(moving, "seq", [(b, a) for a, b in seq_next])

    quarter = half_rows // 2

    def spread(moving):
        return [step(moving), step_back(moving)]

    def pass_on(received):
        return [step(received[0][:quarter]), step_back(received[1][quarter:])]

    mod_half, table_rows, extra = first_call(
        step_index, core[None], hidden_state, modulation.transpose(1, 0, 2), adjoint_rows, text_kv[0]
    )
    mod_near = spread(mod_half)

    w_qkv, w_out, mod_half = pin((w_qkv, w_out, mod_half))
    take = lambda c: lax.dynamic_slice(w_qkv, (0, c, window * HD), (shard, 1, inner))[:, 0]
    own_w = [
        jnp.concatenate([take(0), take(1)], axis=1),
        jnp.concatenate([take(2), lax.dynamic_slice_in_dim(w_out, window * HD, inner, 0).T], axis=1),
    ]
    w_first = [lax.ppermute(part, ("dp", "head"), first_way) for part in own_w]
    w_second = [lax.ppermute(part, ("dp", "head"), second_way) for part in own_w]

    text_dev = text_kv.shape[1]
    mod_far = pass_on(mod_near)
    clip_limit = 0.5 * (tok_count * seq_count * model_width) ** 0.5
    extra, *w_first = pin((extra, *w_first))
    cotangent, cot_half, base = cotangent_call(
        clip_limit, scalars, adjoint_rows, table_rows, text_kv[0], extra, *mod_near, mod_far[1]
    )
    cot_half, mod_far[0] = pin((cot_half, mod_far[0]))
    cot_near = spread(cot_half)
    modulated, normed_share, scale_share, inv_std = local_call(
        modulate_kernel,
        [
            ((tok_count, model_width + EXTRA), bf16),
            ((tok_count, half_width), f32),
            ((1, half_width), f32),
            ((tok_count, 128), f32),
        ],
        1,
        core[None],
        hidden_state,
        table_rows,
        extra,
    )
    def pieces(own, received):
        return [own] + [one for moved in received for one in (moved, other_core(moved))]

    mod_far = list(pin((*mod_far, modulated))[:2])
    mod_pieces = pieces(modulated, mod_near + mod_far)
    w_diagonal = [lax.ppermute(part, ("dp", "head"), second_way) for part in w_first]
    weights = [part[n] for n in range(2) for part in (own_w, w_first, w_second, w_diagonal)]
    cot_near[0] = pin((cot_near[0], w_second, w_diagonal))[0]
    cot_far = [step(cot_near[0])]

    cot_pieces = pieces(cotangent, cot_near)
    *cot_pieces, mod_pieces[-1] = pin((*cot_pieces, mod_pieces[-1]))
    *operands, w_keep, w_give = project_call(
        scalars, qk_gain, mod_pieces, weights, slots, tok_count, text_dev, seq_count
    )
    w_give, cot_far[0] = pin((w_give, *cot_far))
    cot_pieces += pieces(None, cot_far)[1:]
    given, *cot_pieces = pin((w_give, *cot_pieces))
    w_other = other_core(given)
    mine, theirs, rest = attend_call(
        scalars, qk_gain, operands + [w_keep, w_give], cot_pieces, weights[4:], slots, tok_count, text_dev
    )
    first = (mine + other_core(theirs).astype(f32)).astype(bf16)
    moving = [first[:half_rows], first[half_rows:]]
    other_rest = other_core(rest)
    rest, other_rest, *_ = pin((rest, other_rest, *moving))
    own = backward_call(rest, other_rest, w_keep, w_other, half_rows, f32)
    for j in range(2, seq_count):
        moving = [step(part) for part in moving]
        moving = [
            (a + b.astype(f32)).astype(bf16) for a, b in zip(own[2 * (j - 2) : 2 * (j - 1)], moving)
        ]
    moving = [step(part) for part in moving]

    grad_scaled, sums = local_call(
        sums_kernel,
        [((tok_count, half_width), f32), ((tok_count, 128), f32)],
        0,
        *own[-2:],
        *moving,
        scale_share,
        normed_share,
    )
    (pulled,) = local_call(
        functools.partial(last_kernel, model_width),
        [((half_width, tok_count), f32)],
        0,
        grad_scaled,
        sums,
        other_core(sums),
        normed_share,
        base,
        inv_std,
    )
    return pulled.T[None]


def qk_normalize(values, gains):
    inverse = lax.rsqrt(jnp.mean(values * values, axis=-1, keepdims=True) + 1e-06)
    return ((values * inverse * gains).astype(jnp.bfloat16), inverse)


def qk_backward(values, inverse, cotangent, gains):
    scaled = cotangent.astype(jnp.float32) * gains
    return (
        scaled * inverse - values * jnp.mean(scaled * values, axis=-1, keepdims=True) * inverse**3
    )


def shards_by_row(states, adjoint, text_kv, text_len, step_index, modulation, w_qkv, qk_gain, w_out):
    hidden_state = states[0]
    adjoint_rows = adjoint[0]
    tok_count, model_width = hidden_state.shape
    seq_count = lax.axis_size("seq")
    inner_dev = w_qkv.shape[2]
    heads_dev = inner_dev // HD
    score_scale = HD ** (-0.5)
    squares = lax.psum(jnp.sum(adjoint_rows * adjoint_rows), "seq")
    clip_limit = 0.5 * (tok_count * seq_count * model_width) ** 0.5
    clip_scale = jnp.minimum(1.0, clip_limit / jnp.sqrt(squares + 1e-06))
    table_row = lax.dynamic_index_in_dim(modulation, step_index[0], 0, keepdims=False)
    offset_row = table_row[0]
    stretch = table_row[1]
    gating = table_row[2]
    widened = hidden_state.astype(jnp.float32)
    centered = widened - jnp.mean(widened, axis=-1, keepdims=True)
    inv_std = lax.rsqrt(jnp.mean(centered * centered, axis=-1, keepdims=True) + 1e-06)
    normed = centered * inv_std
    modulated = (normed * (1.0 + stretch) + offset_row).astype(jnp.bfloat16)
    cotangent = (gating * (clip_scale * adjoint_rows)).astype(jnp.bfloat16)
    contract_last = (((1,), (1,)), ((), ()))
    full_weight = lax.all_gather(w_qkv, "dp", axis=0, tiled=True).reshape(
        model_width, 3 * inner_dev
    )
    projected = jnp.dot(modulated, full_weight, preferred_element_type=jnp.float32)
    out_raw = lax.dot_general(
        cotangent,
        lax.all_gather(w_out, "dp", axis=1, tiled=True),
        contract_last,
        preferred_element_type=jnp.float32,
    )
    projected = projected.reshape(tok_count, 3, heads_dev, HD)
    queries, query_inv = qk_normalize(projected[:, 0], qk_gain[0])
    own_keys, key_inv = qk_normalize(projected[:, 1], qk_gain[1])
    own_values = projected[:, 2].astype(jnp.bfloat16)
    out_grad = out_raw.astype(jnp.bfloat16).reshape(tok_count, heads_dev, HD)
    text_keys = text_kv[0, :, 0, :]
    text_values = text_kv[0, :, 1, :]
    text_dev = text_keys.shape[0]
    rows_dev = tok_count + text_dev
    key_local = jnp.concatenate([own_keys.reshape(tok_count, inner_dev), text_keys], axis=0)
    value_local = jnp.concatenate([own_values.reshape(tok_count, inner_dev), text_values], axis=0)
    key_all, value_all = (
        lax.all_gather(key_local, "seq", axis=0, tiled=True),
        lax.all_gather(value_local, "seq", axis=0, tiled=True),
    )
    all_rows = rows_dev * seq_count
    row_ids = jnp.arange(all_rows, dtype=jnp.int32)
    owner = row_ids // rows_dev
    within = row_ids % rows_dev
    allowed = (within < tok_count) | (owner * text_dev + within - tok_count < text_len[0])
    group = 1
    while group * 2 * rows_dev <= 512 and seq_count % (group * 2) == 0:
        group = group * 2
    block_rows = group * rows_dev
    block_count = all_rows // block_rows
    key_blocks = key_all.reshape(block_count, block_rows, heads_dev, HD)
    value_blocks = value_all.reshape(block_count, block_rows, heads_dev, HD)
    mask_blocks = allowed.reshape(block_count, block_rows)

    def block_scores(key_block, mask_block):
        scores = (
            jnp.einsum("qhd,khd->qhk", queries, key_block, preferred_element_type=jnp.float32)
            * score_scale
        )
        return jnp.where(mask_block[None, None, :], scores, -1e30)

    def first_pass(carry, block):
        row_max, row_sum, row_dot = carry
        key_block, value_block, mask_block = block
        scores = block_scores(key_block, mask_block)
        new_max = jnp.maximum(row_max, jnp.max(scores, axis=-1))
        rescale = jnp.exp(row_max - new_max)
        exps = jnp.exp(scores - new_max[:, :, None])
        grad_weights = jnp.einsum(
            "qhd,khd->qhk", out_grad, value_block, preferred_element_type=jnp.float32
        )
        return (
            (
                new_max,
                row_sum * rescale + jnp.sum(exps, axis=-1),
                row_dot * rescale + jnp.sum(exps * grad_weights, axis=-1),
            ),
            None,
        )

    start_state = (
        jnp.full((tok_count, heads_dev), -1e30, jnp.float32),
        jnp.zeros((tok_count, heads_dev), jnp.float32),
        jnp.zeros((tok_count, heads_dev), jnp.float32),
    )
    (row_max, row_sum, row_dot), unused = lax.scan(
        first_pass, start_state, (key_blocks, value_blocks, mask_blocks)
    )
    log_total = row_max + jnp.log(row_sum)
    delta_row = row_dot / row_sum

    def second_pass(running, block):
        key_block, value_block, mask_block = block
        weights = jnp.exp(block_scores(key_block, mask_block) - log_total[:, :, None])
        grad_weights = jnp.einsum(
            "qhd,khd->qhk", out_grad, value_block, preferred_element_type=jnp.float32
        )
        grad_scores = (weights * (grad_weights - delta_row[:, :, None])).astype(jnp.bfloat16)
        return (
            running
            + jnp.einsum(
                "qhk,khd->qhd", grad_scores, key_block, preferred_element_type=jnp.float32
            ),
            None,
        )

    query_sum, unused = lax.scan(
        second_pass,
        jnp.zeros((tok_count, heads_dev, HD), jnp.float32),
        (key_blocks, value_blocks, mask_blocks),
    )
    grad_query = (query_sum * score_scale).astype(jnp.bfloat16)
    log_all, delta_all = (
        lax.all_gather(log_total, "seq", axis=0, tiled=True),
        lax.all_gather(delta_row, "seq", axis=0, tiled=True),
    )
    local_ids = jnp.arange(rows_dev, dtype=jnp.int32)
    local_allowed = (local_ids < tok_count) | (
        lax.axis_index("seq") * text_dev + local_ids - tok_count < text_len[0]
    )
    key_three = key_local.reshape(rows_dev, heads_dev, HD)
    value_three = value_local.reshape(rows_dev, heads_dev, HD)
    query_piece = lax.all_gather(queries.reshape(tok_count, inner_dev), "seq", axis=0, tiled=True)
    grad_piece = lax.all_gather(out_grad.reshape(tok_count, inner_dev), "seq", axis=0, tiled=True)
    piece_rows = query_piece.shape[0]
    query_rows = query_piece.reshape(piece_rows, heads_dev, HD)
    grad_rows = grad_piece.reshape(piece_rows, heads_dev, HD)
    scores = (
        jnp.einsum("qhd,khd->qhk", query_rows, key_three, preferred_element_type=jnp.float32)
        * score_scale
    )
    scores = jnp.where(local_allowed[None, None, :], scores, -1e30)
    weights = jnp.exp(scores - log_all[:, :, None])
    grad_weights = jnp.einsum(
        "qhd,khd->qhk", grad_rows, value_three, preferred_element_type=jnp.float32
    )
    grad_scores = (weights * (grad_weights - delta_all[:, :, None])).astype(jnp.bfloat16)
    rounded = weights.astype(jnp.bfloat16)
    key_sum = jnp.einsum(
        "qhk,qhd->khd", grad_scores, query_rows, preferred_element_type=jnp.float32
    )
    value_sum = jnp.einsum("qhk,qhd->khd", rounded, grad_rows, preferred_element_type=jnp.float32)
    key_sum, value_sum = (key_sum, value_sum)
    grad_key = (key_sum[:tok_count] * score_scale).astype(jnp.bfloat16)
    grad_value = value_sum[:tok_count].astype(jnp.bfloat16)
    raw_query = qk_backward(projected[:, 0], query_inv, grad_query, qk_gain[0])
    raw_key = qk_backward(projected[:, 1], key_inv, grad_key, qk_gain[1])
    stacked = jnp.stack([raw_query, raw_key, grad_value.astype(jnp.float32)], axis=1).astype(
        jnp.bfloat16
    )
    stacked = stacked.reshape(tok_count, 3 * inner_dev)
    partial_grad = lax.dot_general(
        stacked, full_weight, contract_last, preferred_element_type=jnp.float32
    )
    half_width = model_width // lax.axis_size("head")
    first_col = lax.axis_index("head") * half_width
    grad_share = lax.psum_scatter(
        partial_grad.astype(jnp.bfloat16), "head", scatter_dimension=1, tiled=True
    ).astype(jnp.float32)
    normed_share = lax.dynamic_slice_in_dim(normed, first_col, half_width, 1)
    stretch_share = lax.dynamic_slice_in_dim(stretch, first_col, half_width, 0)
    adjoint_share = lax.dynamic_slice_in_dim(adjoint_rows, first_col, half_width, 1)
    grad_scaled = grad_share * (1.0 + stretch_share)
    row_sums = jnp.stack(
        [jnp.sum(grad_scaled, axis=-1), jnp.sum(grad_scaled * normed_share, axis=-1)], axis=-1
    )
    row_sums = lax.psum(row_sums, "head")
    grad_state = inv_std * (
        grad_scaled - row_sums[:, 0:1] / model_width - normed_share * row_sums[:, 1:2] / model_width
    )
    pulled = clip_scale * adjoint_share + grad_state
    return pulled[None]


def solution(mesh):
    in_specs = (
        P("dp", "seq", None),
        P("dp", "seq", None),
        P("dp", "seq", None, "head"),
        P("dp"),
        P("dp"),
        P(),
        P("dp", None, "head"),
        P(),
        P("head", "dp"),
    )
    out_specs = P("dp", "seq", "head")
    by_head = mesh.shape["seq"] == 4 and mesh.shape["dp"] == 4 and mesh.shape["head"] == 2
    shards = shards_by_head if by_head else shards_by_row
    return jax.shard_map(shards, mesh=mesh, in_specs=in_specs, out_specs=out_specs, check_vma=False)
```

profile of v0, /device:TPU:0, one launch (start us, length us, event | category | flops | bytes accessed | tf_op | source)
XLA Modules:
  0.0 109.4 jit_solution(3364745374834124439)
XLA Ops:
  0.7 2.9 %shard_map.91 = (bf16[64,2560]{1,0:T(8,128)(2,1)}, f32[8,2432]{1,0:T(8,128)}, bf16[64,128]{1,0:T(8,128)(2,1)}) custom-call(s32[1]{0:T(128)S(6)} %copy.11.step, s32[1]{0:T(128)} %bitcast.core, bf16[128,2432]{1,0:T(8,128)(2,1)} %bitcast.30, f32[3,28,2432]{2,1,0:T(8,128)} %bitcast.34, f32[128,2432]{1,0:T(8,128)} %bitcast.28, bf16[8,2,640]{2,1,0:T(2,128)(2,1)} %bitcast.32), custom_call_target="tpu_custom_call" | custom-call | flops 1245184 | bytes 2490368 | tf_op jit(solution)/shard_map/pallas_call | solution.py:110
  3.6 4.0 %collective-permute-start.4 = (bf16[64,2560]{1,0:T(8,128)(2,1)}, bf16[64,2560]{1,0:T(8,128)(2,1)S(1)}, u32[]{:S(2)}, u32[]{:S(2)}) collective-permute-start(bf16[64,2560]{1,0:T(8,128)(2,1)} %get-tuple-element.64), channel_id=1, source_target_pairs={{2,0},{6,2},{4,6},{0,4},{3,1},{7,3},{5,7},{1,5},{10,8},{14,10},{12... | collective-permute-start | bytes 983048 | tf_op jit(solution)/shard_map/ppermute | solution.py:571
  7.6 1.7 %dynamic-slice_bitcast_fusion.1 = (bf16[608,192]{1,0:T(8,128)(2,1)S(1)}, bf16[608,192]{1,0:T(8,128)(2,1)S(1)}, bf16[608,192]{1,0:T(8,128)(2,1)S(1)}) fusion(bf16[608,3,640]{2,0,1:T(8,128)(2,1)} %param.15, s32[]{:T(128)S(6)} %select_n.103), kind=kLoop, calls=%fused_computation.8 | loop fusion | bytes 1400836 | tf_op jit(solution)/shard_map/squeeze | solution.py:587
  9.3 0.2 dynamic-slice_bitcast_fusion
  9.5 1.0 pad_maximum_fusion.1.refs_13_.refs_15_
  10.5 1.5 %collective-permute-start.1 = (bf16[608,384]{1,0:T(8,128)(2,1)}, bf16[608,384]{1,0:T(8,128)(2,1)}, u32[]{:S(2)}, u32[]{:S(2)}) collective-permute-start(bf16[608,384]{1,0:T(8,128)(2,1)} %pad_maximum_fusion.1.refs_13_.refs_15_), channel_id=1, source_target_pairs={{0,8},{1,17},{8,0},{9,25},{16,24},{17,1},{24,16},{25,9},{2,10},{3,... | collective-permute-start | bytes 1400840 | tf_op jit(solution)/shard_map/ppermute | solution.py:592
  12.0 0.9 pad_maximum_fusion.refs_9_
  12.9 0.5 collective-permute-start
  13.5 1.5 %collective-permute-start.11 = (bf16[608,384]{1,0:T(8,128)(2,1)}, bf16[608,384]{1,0:T(8,128)(2,1)}, u32[]{:S(2)}, u32[]{:S(2)}) collective-permute-start(bf16[608,384]{1,0:T(8,128)(2,1)} %pad_maximum_fusion.1.refs_13_.refs_15_), channel_id=1, source_target_pairs={{0,16},{1,9},{8,24},{9,1},{16,0},{17,25},{24,8},{25,17},{2,18},{3,... | collective-permute-start | bytes 1400840 | tf_op jit(solution)/shard_map/ppermute | solution.py:593
  15.0 1.1 collective-permute-done.4.following.refs_3_
  16.1 0.7 slice.16
  16.8 3.3 %collective-permute-start.6 = (bf16[32,2560]{1,0:T(8,128)(2,1)}, bf16[32,2560]{1,0:T(8,128)(2,1)S(1)}, u32[]{:S(2)}, u32[]{:S(2)}) collective-permute-start(bf16[32,2560]{1,0:T(8,128)(2,1)} %slice.16), channel_id=1, source_target_pairs={{2,0},{6,2},{4,6},{0,4},{3,1},{7,3},{5,7},{1,5},{10,8},{14,10},{12... | collective-permute-start | bytes 491528 | tf_op jit(solution)/shard_map/ppermute | solution.py:571
  20.1 4.7 %collective-permute-done.2.previous.refs_1_ = bf16[64,2560]{1,0:T(8,128)(2,1)S(1)} collective-permute-done((bf16[64,2560]{1,0:T(8,128)(2,1)}, bf16[64,2560]{1,0:T(8,128)(2,1)S(1)}, u32[]{:S(2)}, u32[]{:S(2)}) %collective-permute-start.2) | collective-permute-done | bytes 327712 | tf_op jit(solution)/shard_map/ppermute | solution.py:565
  24.8 0.7 slice.17
  25.5 0.7 collective-permute-start.7
  26.2 1.5 %collective-permute-start.10 = (bf16[608,384]{1,0:T(8,128)(2,1)}, bf16[608,384]{1,0:T(8,128)(2,1)}, u32[]{:S(2)}, u32[]{:S(2)}) collective-permute-start(bf16[608,384]{1,0:T(8,128)(2,1)} %pad_maximum_fusion.refs_9_), channel_id=1, source_target_pairs={{0,16},{1,9},{8,24},{9,1},{16,0},{17,25},{24,8},{25,17},{2,18},{3,... | collective-permute-start | bytes 1400840 | tf_op jit(solution)/shard_map/ppermute | solution.py:593
  28.5 1.8 %collective-permute-done.refs_10_ = bf16[608,384]{1,0:T(8,128)(2,1)} collective-permute-done((bf16[608,384]{1,0:T(8,128)(2,1)}, bf16[608,384]{1,0:T(8,128)(2,1)}, u32[]{:S(2)}, u32[]{:S(2)}) %collective-permute-start) | collective-permute-done | bytes 466976 | tf_op jit(solution)/shard_map/ppermute | solution.py:592
  30.4 0.8 copy-done.12
  31.2 0.7 copy-done.13
  31.9 0.9 shard_map.93
  32.8 0.8 copy-done.6
  33.7 0.8 copy-done.8
  34.5 3.2 %collective-permute-start.15 = (bf16[64,2560]{1,0:T(8,128)(2,1)S(1)}, bf16[64,2560]{1,0:T(8,128)(2,1)S(1)}, u32[]{:S(2)}, u32[]{:S(2)}) collective-permute-start(bf16[64,2560]{1,0:T(8,128)(2,1)S(1)} %get-tuple-element.74), channel_id=1, source_target_pairs={{2,0},{6,2},{4,6},{0,4},{3,1},{7,3},{5,7},{1,5},{10,8},{14,10},{12... | collective-permute-start | bytes 983048 | tf_op jit(solution)/shard_map/ppermute | solution.py:571
  37.7 1.5 %collective-permute-start.12 = (bf16[608,384]{1,0:T(8,128)(2,1)}, bf16[608,384]{1,0:T(8,128)(2,1)S(1)}, u32[]{:S(2)}, u32[]{:S(2)}) collective-permute-start(bf16[608,384]{1,0:T(8,128)(2,1)} %collective-permute-done.refs_10_), channel_id=1, source_target_pairs={{0,16},{1,9},{8,24},{9,1},{16,0},{17,25},{24,8},{25,17},{2,18},{3,... | collective-permute-start | bytes 1400840 | tf_op jit(solution)/shard_map/ppermute | solution.py:623
  39.2 0.5 collective-permute-start.13
  39.8 5.8 %collective-permute-done.15.refs_11_ = bf16[64,2560]{1,0:T(8,128)(2,1)S(1)} collective-permute-done((bf16[64,2560]{1,0:T(8,128)(2,1)S(1)}, bf16[64,2560]{1,0:T(8,128)(2,1)S(1)}, u32[]{:S(2)}, u32[]{:S(2)}) %collective-permute-start.15) | collective-permute-done | bytes 327712 | tf_op jit(solution)/shard_map/ppermute | solution.py:571
  45.6 0.6 shard_map.92
  46.1 0.8 copy-done.10
  47.0 0.5 collective-permute-start.17
  47.5 4.0 %collective-permute-done.9.refs_9_ = bf16[64,2560]{1,0:T(8,128)(2,1)} collective-permute-done((bf16[64,2560]{1,0:T(8,128)(2,1)S(1)}, bf16[64,2560]{1,0:T(8,128)(2,1)}, u32[]{:S(2)}, u32[]{:S(2)}) %collective-permute-start.9) | collective-permute-done | bytes 327712 | tf_op jit(solution)/shard_map/ppermute | solution.py:565
  51.6 0.5 collective-permute-start.3
  52.2 0.3 collective-permute-start.18
  52.5 0.2 collective-permute-start.8
  52.7 0.7 collective-permute-done.14.refs_10_
  53.4 1.2 %collective-permute-done.8.refs_6_ = bf16[32,2560]{1,0:T(8,128)(2,1)S(1)} collective-permute-done((bf16[32,2560]{1,0:T(8,128)(2,1)}, bf16[32,2560]{1,0:T(8,128)(2,1)S(1)}, u32[]{:S(2)}, u32[]{:S(2)}) %collective-permute-start.8) | collective-permute-done | bytes 163872 | tf_op jit(solution)/shard_map/ppermute | solution.py:568
  54.6 0.6 copy-done.25
  55.3 0.7 copy-done.22
  56.0 8.5 %shard_map.94 = (bf16[512,576]{1,0:T(8,128)(2,1)}, bf16[192,512]{1,0:T(8,128)(2,1)}, f32[512,384]{1,0:T(8,128)}, f32[512,384]{1,0:T(8,128)}, bf16[3,32,64]{2,1,0...) custom-call(s32[14]{0:T(128)} %copy-done.14, f32[2,64]{1,0:T(2,128)} %gain.3, ...), custom_call_target="tpu_custom_call" | custom-call | flops 1434451968 | bytes 7798784 | tf_op jit(solution)/shard_map/pallas_call | solution.py:413
  64.5 0.2 collective-permute-start.19
  64.6 0.5 copy-done.21
  65.2 1.0 collective-permute-done.19.refs_14_
  66.3 0.6 copy-done.23
  66.9 11.0 %shard_map.95 = (f32[128,1216]{1,0:T(8,128)}, bf16[128,1216]{1,0:T(8,128)(2,1)}, bf16[384,640]{1,0:T(8,128)(2,1)}) custom-call(s32[14]{0:T(128)} %copy-done.14, f32[2,64]{1,0:T(2,128)} %gain.3, bf16[512,576]{1,0:T(8,128)(2,1)} %get-tuple-element.79.refs_0_, bf16[192,512]{1,0:T(8,128)(2,1)} %get-tuple-element.80.refs_1_, ...), custom_call_target="tpu_custom_call" | custom-call | flops 981467136 | bytes 4358144 | tf_op jit(solution)/shard_map/pallas_call | solution.py:444
  77.9 0.2 collective-permute-start.21
  78.1 0.4 collective-permute-start.20
  78.5 1.3 %collective-permute-done.21 = bf16[128,1216]{1,0:T(8,128)(2,1)S(1)} collective-permute-done((bf16[128,1216]{1,0:T(8,128)(2,1)}, bf16[128,1216]{1,0:T(8,128)(2,1)S(1)}, u32[]{:S(2)}, u32[]{:S(2)}) %collective-permute-start.21) | collective-permute-done | bytes 311328 | tf_op jit(solution)/shard_map/ppermute | solution.py:568
  79.8 1.1 %add_convert_fusion = bf16[128,1216]{1,0:T(8,128)(2,1)S(1)} fusion(f32[128,1216]{1,0:T(8,128)} %get-tuple-element.102, bf16[128,1216]{1,0:T(8,128)(2,1)S(1)} %collective-permute-done.21), kind=kLoop, calls=%fused_computation | loop fusion | flops 466944 | bytes 1245184 | tf_op jit(solution)/shard_map/convert_element_type | solution.py:640
  81.0 2.0 %collective-permute-start.26 = (bf16[64,1216]{1,0:T(8,128)(2,1)S(1)}, bf16[64,1216]{1,0:T(8,128)(2,1)S(1)}, u32[]{:S(2)}, u32[]{:S(2)}) collective-permute-start(bf16[64,1216]{1,0:T(8,128)(2,1)S(1)} %get-tuple-element.122), channel_id=1, source_target_pairs={{0,2},{2,6},{6,4},{4,0},{1,3},{3,7},{7,5},{5,1},{8,10},{10,14},{14... | collective-permute-start | bytes 466952 | tf_op jit(solution)/shard_map/ppermute | solution.py:565
  82.9 0.4 collective-permute-start.23
  83.4 1.0 copy-done.15
  84.4 1.7 %shard_map.96 = (f32[64,1216]{1,0:T(8,128)S(1)}, f32[64,1216]{1,0:T(8,128)S(1)}, f32[64,1216]{1,0:T(8,128)S(1)}, f32[64,1216]{1,0:T(8,128)S(1)}, f32[64,1216]{1,0:T(8,128)S(1)}, /*index=5*/f32[64,1216]{1,0:T(8,128)S(1)}) custom-call(bf16[384,640]{1,0:T(8,128)(2,1)S(1)} %copy-done.15, bf16[384,640]{1,0:T(8,128)(2,1)S(1)} %collective-permute-done.20.other, ...), custom_call_target="tpu_custom_call" | custom-call | flops 1195376640 | bytes 5963776 | tf_op jit(solution)/shard_map/pallas_call | solution.py:480
  86.1 2.9 %collective-permute-done.26 = bf16[64,1216]{1,0:T(8,128)(2,1)S(1)} collective-permute-done((bf16[64,1216]{1,0:T(8,128)(2,1)S(1)}, bf16[64,1216]{1,0:T(8,128)(2,1)S(1)}, u32[]{:S(2)}, u32[]{:S(2)}) %collective-permute-start.26) | collective-permute-done | bytes 155680 | tf_op jit(solution)/shard_map/ppermute | solution.py:565
  89.0 1.1 collective-permute-start.27
  90.1 2.2 %collective-permute-done.23 = bf16[64,1216]{1,0:T(8,128)(2,1)S(1)} collective-permute-done((bf16[64,1216]{1,0:T(8,128)(2,1)S(1)}, bf16[64,1216]{1,0:T(8,128)(2,1)S(1)}, u32[]{:S(2)}, u32[]{:S(2)}) %collective-permute-start.23) | collective-permute-done | bytes 155680 | tf_op jit(solution)/shard_map/ppermute | solution.py:565
  92.3 1.3 %collective-permute-start.24 = (bf16[64,1216]{1,0:T(8,128)(2,1)S(1)}, bf16[64,1216]{1,0:T(8,128)(2,1)S(1)}, u32[]{:S(2)}, u32[]{:S(2)}) collective-permute-start(bf16[64,1216]{1,0:T(8,128)(2,1)S(1)} %add_convert_fusion.4), channel_id=1, source_target_pairs={{0,2},{2,6},{6,4},{4,0},{1,3},{3,7},{7,5},{5,1},{8,10},{10,14},{14... | collective-permute-start | bytes 466952 | tf_op jit(solution)/shard_map/ppermute | solution.py:565
  93.6 2.4 %collective-permute-done.27 = bf16[64,1216]{1,0:T(8,128)(2,1)S(1)} collective-permute-done((bf16[64,1216]{1,0:T(8,128)(2,1)S(1)}, bf16[64,1216]{1,0:T(8,128)(2,1)S(1)}, u32[]{:S(2)}, u32[]{:S(2)}) %collective-permute-start.27) | collective-permute-done | bytes 155680 | tf_op jit(solution)/shard_map/ppermute | solution.py:565
  96.0 1.3 %collective-permute-start.28 = (bf16[64,1216]{1,0:T(8,128)(2,1)S(1)}, bf16[64,1216]{1,0:T(8,128)(2,1)S(1)}, u32[]{:S(2)}, u32[]{:S(2)}) collective-permute-start(bf16[64,1216]{1,0:T(8,128)(2,1)S(1)} %add_convert_fusion.1), channel_id=1, source_target_pairs={{0,2},{2,6},{6,4},{4,0},{1,3},{3,7},{7,5},{5,1},{8,10},{10,14},{14... | collective-permute-start | bytes 466952 | tf_op jit(solution)/shard_map/ppermute | solution.py:565
  97.3 3.1 %collective-permute-done.24 = bf16[64,1216]{1,0:T(8,128)(2,1)S(1)} collective-permute-done((bf16[64,1216]{1,0:T(8,128)(2,1)S(1)}, bf16[64,1216]{1,0:T(8,128)(2,1)S(1)}, u32[]{:S(2)}, u32[]{:S(2)}) %collective-permute-start.24) | collective-permute-done | bytes 155680 | tf_op jit(solution)/shard_map/ppermute | solution.py:565
  100.4 0.4 collective-permute-start.25
  100.8 3.0 %collective-permute-done.28.far = bf16[64,1216]{1,0:T(8,128)(2,1)S(1)} collective-permute-done((bf16[64,1216]{1,0:T(8,128)(2,1)S(1)}, bf16[64,1216]{1,0:T(8,128)(2,1)S(1)}, u32[]{:S(2)}, u32[]{:S(2)}) %collective-permute-start.28) | collective-permute-done | bytes 155680 | tf_op jit(solution)/shard_map/ppermute | solution.py:565
  103.8 2.9 %collective-permute-done.25.near = bf16[64,1216]{1,0:T(8,128)(2,1)S(1)} collective-permute-done((bf16[64,1216]{1,0:T(8,128)(2,1)S(1)}, bf16[64,1216]{1,0:T(8,128)(2,1)S(1)}, u32[]{:S(2)}, u32[]{:S(2)}) %collective-permute-start.25) | collective-permute-done | bytes 155680 | tf_op jit(solution)/shard_map/ppermute | solution.py:565
  106.7 0.2 shard_map.97
  107.0 1.2 %collective-permute-done.29.other = f32[128,128]{1,0:T(8,128)S(1)} collective-permute-done((f32[128,128]{1,0:T(8,128)S(1)}, f32[128,128]{1,0:T(8,128)S(1)}, u32[]{:S(2)}, u32[]{:S(2)}) %collective-permute-start.29) | collective-permute-done | bytes 65568 | tf_op jit(solution)/shard_map/ppermute | solution.py:568
  108.2 1.2 %shard_map.98 = f32[1216,128]{1,0:T(8,128)} custom-call(f32[128,1216]{1,0:T(8,128)S(1)} %get-tuple-element.115.grad, f32[128,128]{1,0:T(8,128)S(1)} %get-tuple-element.116.sums, f32[128,128]{1,0:T(8,128)S(1)} %collective-permute-done.29.other, f32[128,1216]{1,0:T(8,128)S(1)} %get-tuple-element.114.normed, f32[128,1216]{1,0:T(8,128)S(1)} %copy-done.9, ...), custom_call_target="tpu_custom_call" | custom-call | flops 516096 | bytes 2064384 | tf_op jit(solution)/shard_map/pallas_call | solution.py:516
  (69 shorter events, 0.7 us)
Async XLA Ops:
  0.0 9.3 %copy-start = (bf16[640,608]{0,1:T(8,128)(2,1)S(1)}, bf16[640,608]{0,1:T(8,128)(2,1)}, u32[]{:S(2)}) copy-start(bf16[640,608]{0,1:T(8,128)(2,1)} %param.17) | copy-start | bytes 2334724
  3.6 12.5 %collective-permute-start.4 = (bf16[64,2560]{1,0:T(8,128)(2,1)}, bf16[64,2560]{1,0:T(8,128)(2,1)S(1)}, u32[]{:S(2)}, u32[]{:S(2)}) collective-permute-start(bf16[64,2560]{1,0:T(8,128)(2,1)} %get-tuple-element.64), channel_id=1, source_target_pairs={{2,0},{6,2},{4,6},{0,4},{3,1},{7,3},{5,7},{1,5},{10,8},{14,10},{12... | collective-permute-start | bytes 983048 | tf_op jit(solution)/shard_map/ppermute | solution.py:571
  7.6 17.2 %collective-permute-start.2 = (bf16[64,2560]{1,0:T(8,128)(2,1)}, bf16[64,2560]{1,0:T(8,128)(2,1)S(1)}, u32[]{:S(2)}, u32[]{:S(2)}) collective-permute-start(bf16[64,2560]{1,0:T(8,128)(2,1)} %get-tuple-element.64), channel_id=1, source_target_pairs={{0,2},{2,6},{6,4},{4,0},{1,3},{3,7},{7,5},{5,1},{8,10},{10,14},{14... | collective-permute-start | bytes 983048 | tf_op jit(solution)/shard_map/ppermute | solution.py:565
  9.5 20.9 %copy-start.1 = (f32[1,128,2432]{2,1,0:T(8,128)S(1)}, f32[1,128,2432]{2,1,0:T(8,128)}, u32[]{:S(2)}) copy-start(f32[1,128,2432]{2,1,0:T(8,128)} %param.10) | copy-start | bytes 3735556
  9.5 20.9 %copy-start.11 = (f32[8,2432]{1,0:T(8,128)S(1)}, f32[8,2432]{1,0:T(8,128)}, u32[]{:S(2)}) copy-start(f32[8,2432]{1,0:T(8,128)} %get-tuple-element.62.table_rows) | copy-start | bytes 233476
  10.5 15.7 %collective-permute-start.1 = (bf16[608,384]{1,0:T(8,128)(2,1)}, bf16[608,384]{1,0:T(8,128)(2,1)}, u32[]{:S(2)}, u32[]{:S(2)}) collective-permute-start(bf16[608,384]{1,0:T(8,128)(2,1)} %pad_maximum_fusion.1.refs_13_.refs_15_), channel_id=1, source_target_pairs={{0,8},{1,17},{8,0},{9,25},{16,24},{17,1},{24,16},{25,9},{2,10},{3,... | collective-permute-start | bytes 1400840 | tf_op jit(solution)/shard_map/ppermute | solution.py:592
  12.9 32.6 %copy-start.2 = (bf16[1,128,2432]{2,1,0:T(8,128)(2,1)S(1)}, bf16[1,128,2432]{2,1,0:T(8,128)(2,1)}, u32[]{:S(2)}) copy-start(bf16[1,128,2432]{2,1,0:T(8,128)(2,1)} %param.9) | copy-start | bytes 1867780
  12.9 17.4 %collective-permute-start = (bf16[608,384]{1,0:T(8,128)(2,1)}, bf16[608,384]{1,0:T(8,128)(2,1)}, u32[]{:S(2)}, u32[]{:S(2)}) collective-permute-start(bf16[608,384]{1,0:T(8,128)(2,1)} %pad_maximum_fusion.refs_9_), channel_id=1, source_target_pairs={{0,8},{1,17},{8,0},{9,25},{16,24},{17,1},{24,16},{25,9},{2,10},{3,... | collective-permute-start | bytes 1400840 | tf_op jit(solution)/shard_map/ppermute | solution.py:592
  13.5 26.3 %collective-permute-start.11 = (bf16[608,384]{1,0:T(8,128)(2,1)}, bf16[608,384]{1,0:T(8,128)(2,1)}, u32[]{:S(2)}, u32[]{:S(2)}) collective-permute-start(bf16[608,384]{1,0:T(8,128)(2,1)} %pad_maximum_fusion.1.refs_13_.refs_15_), channel_id=1, source_target_pairs={{0,16},{1,9},{8,24},{9,1},{16,0},{17,25},{24,8},{25,17},{2,18},{3,... | collective-permute-start | bytes 1400840 | tf_op jit(solution)/shard_map/ppermute | solution.py:593
  16.1 36.0 %copy-start.3 = (bf16[64,2560]{1,0:T(8,128)(2,1)}, bf16[64,2560]{1,0:T(8,128)(2,1)S(1)}, u32[]{:S(2)}) copy-start(bf16[64,2560]{1,0:T(8,128)(2,1)S(1)} %collective-permute-done.4.following.refs_3_) | copy-start | bytes 983044
  16.8 13.6 %collective-permute-start.6 = (bf16[32,2560]{1,0:T(8,128)(2,1)}, bf16[32,2560]{1,0:T(8,128)(2,1)S(1)}, u32[]{:S(2)}, u32[]{:S(2)}) collective-permute-start(bf16[32,2560]{1,0:T(8,128)(2,1)} %slice.16), channel_id=1, source_target_pairs={{2,0},{6,2},{4,6},{0,4},{3,1},{7,3},{5,7},{1,5},{10,8},{14,10},{12... | collective-permute-start | bytes 491528 | tf_op jit(solution)/shard_map/ppermute | solution.py:571
  24.8 26.7 %copy-start.4 = (bf16[64,2560]{1,0:T(8,128)(2,1)}, bf16[64,2560]{1,0:T(8,128)(2,1)S(1)}, u32[]{:S(2)}) copy-start(bf16[64,2560]{1,0:T(8,128)(2,1)S(1)} %collective-permute-done.2.previous.refs_1_) | copy-start | bytes 983044
  25.5 9.0 %collective-permute-start.7 = (bf16[32,2560]{1,0:T(8,128)(2,1)}, bf16[32,2560]{1,0:T(8,128)(2,1)}, u32[]{:S(2)}, u32[]{:S(2)}) collective-permute-start(bf16[32,2560]{1,0:T(8,128)(2,1)} %slice.17), channel_id=1, source_target_pairs={{0,2},{2,6},{6,4},{4,0},{1,3},{3,7},{7,5},{5,1},{8,10},{10,14},{14... | collective-permute-start | bytes 491528 | tf_op jit(solution)/shard_map/ppermute | solution.py:565
  26.2 20.8 %collective-permute-start.10 = (bf16[608,384]{1,0:T(8,128)(2,1)}, bf16[608,384]{1,0:T(8,128)(2,1)}, u32[]{:S(2)}, u32[]{:S(2)}) collective-permute-start(bf16[608,384]{1,0:T(8,128)(2,1)} %pad_maximum_fusion.refs_9_), channel_id=1, source_target_pairs={{0,16},{1,9},{8,24},{9,1},{16,0},{17,25},{24,8},{25,17},{2,18},{3,... | collective-permute-start | bytes 1400840 | tf_op jit(solution)/shard_map/ppermute | solution.py:593
  28.5 26.7 %copy-start.14 = (s32[14]{0:T(128)}, s32[14]{0:T(128)S(1)}, u32[]{:S(2)}) copy-start(s32[14]{0:T(128)S(1)} %stack.67.core.scalars) | copy-start | bytes 172
  30.4 24.9 %copy-start.7 = (bf16[32,2560]{1,0:T(8,128)(2,1)}, bf16[32,2560]{1,0:T(8,128)(2,1)S(1)}, u32[]{:S(2)}) copy-start(bf16[32,2560]{1,0:T(8,128)(2,1)S(1)} %collective-permute-done.6.opposite.refs_7_) | copy-start | bytes 491524
  30.4 0.8 copy-start.12
  31.2 0.7 copy-start.13
  32.8 0.8 copy-start.6
  33.7 0.8 copy-start.8
  34.5 11.0 %collective-permute-start.15 = (bf16[64,2560]{1,0:T(8,128)(2,1)S(1)}, bf16[64,2560]{1,0:T(8,128)(2,1)S(1)}, u32[]{:S(2)}, u32[]{:S(2)}) collective-permute-start(bf16[64,2560]{1,0:T(8,128)(2,1)S(1)} %get-tuple-element.74), channel_id=1, source_target_pairs={{2,0},{6,2},{4,6},{0,4},{3,1},{7,3},{5,7},{1,5},{10,8},{14,10},{12... | collective-permute-start | bytes 983048 | tf_op jit(solution)/shard_map/ppermute | solution.py:571
  37.7 13.7 %collective-permute-start.12 = (bf16[608,384]{1,0:T(8,128)(2,1)}, bf16[608,384]{1,0:T(8,128)(2,1)S(1)}, u32[]{:S(2)}, u32[]{:S(2)}) collective-permute-start(bf16[608,384]{1,0:T(8,128)(2,1)} %collective-permute-done.refs_10_), channel_id=1, source_target_pairs={{0,16},{1,9},{8,24},{9,1},{16,0},{17,25},{24,8},{25,17},{2,18},{3,... | collective-permute-start | bytes 1400840 | tf_op jit(solution)/shard_map/ppermute | solution.py:623
  39.2 12.3 %collective-permute-start.13 = (bf16[608,384]{1,0:T(8,128)(2,1)}, bf16[608,384]{1,0:T(8,128)(2,1)S(1)}, u32[]{:S(2)}, u32[]{:S(2)}) collective-permute-start(bf16[608,384]{1,0:T(8,128)(2,1)} %collective-permute-done.1.refs_14_.refs_16_), channel_id=1, source_target_pairs={{0,16},{1,9},{8,24},{9,1},{16,0},{17,25},{24,8},{25,17},{2,18},{3,... | collective-permute-start | bytes 1400840 | tf_op jit(solution)/shard_map/ppermute | solution.py:623
  39.8 11.7 %collective-permute-start.9 = (bf16[64,2560]{1,0:T(8,128)(2,1)S(1)}, bf16[64,2560]{1,0:T(8,128)(2,1)}, u32[]{:S(2)}, u32[]{:S(2)}) collective-permute-start(bf16[64,2560]{1,0:T(8,128)(2,1)S(1)} %get-tuple-element.74), channel_id=1, source_target_pairs={{0,2},{2,6},{6,4},{4,0},{1,3},{3,7},{7,5},{5,1},{8,10},{10,14},{14... | collective-permute-start | bytes 983048 | tf_op jit(solution)/shard_map/ppermute | solution.py:565
  45.5 9.0 %copy-start.18 = (bf16[64,2560]{1,0:T(8,128)(2,1)}, bf16[64,2560]{1,0:T(8,128)(2,1)S(1)}, u32[]{:S(2)}) copy-start(bf16[64,2560]{1,0:T(8,128)(2,1)S(1)} %collective-permute-done.15.refs_11_) | copy-start | bytes 983044
  45.6 7.0 %collective-permute-start.16 = (bf16[64,2560]{1,0:T(8,128)(2,1)S(1)}, bf16[64,2560]{1,0:T(8,128)(2,1)S(1)}, u32[]{:S(2)}, u32[]{:S(2)}) collective-permute-start(bf16[64,2560]{1,0:T(8,128)(2,1)S(1)} %collective-permute-done.15.refs_11_), channel_id=1, source_target_pairs={{0,1},{1,0},{2,3},{3,2},{4,5},{5,4},{6,7},{7,6},{8,9},{9,8},{10,11... | collective-permute-start | bytes 983048 | tf_op jit(solution)/shard_map/ppermute | solution.py:568
  46.1 0.9 copy-start.10
  47.0 5.2 %collective-permute-start.17 = (bf16[32,2560]{1,0:T(8,128)(2,1)S(1)}, bf16[32,2560]{1,0:T(8,128)(2,1)S(1)}, u32[]{:S(2)}, u32[]{:S(2)}) collective-permute-start(bf16[32,2560]{1,0:T(8,128)(2,1)S(1)} %collective-permute-done.6.opposite.refs_7_), channel_id=1, source_target_pairs={{0,1},{1,0},{2,3},{3,2},{4,5},{5,4},{6,7},{7,6},{8,9},{9,8},{10,11... | collective-permute-start | bytes 491528 | tf_op jit(solution)/shard_map/ppermute | solution.py:568
  51.5 3.1 %copy-start.17 = (bf16[608,384]{1,0:T(8,128)(2,1)}, bf16[608,384]{1,0:T(8,128)(2,1)S(1)}, u32[]{:S(2)}) copy-start(bf16[608,384]{1,0:T(8,128)(2,1)S(1)} %collective-permute-done.12.refs_12_) | copy-start | bytes 1400836
  51.5 3.7 %copy-start.16 = (bf16[608,384]{1,0:T(8,128)(2,1)}, bf16[608,384]{1,0:T(8,128)(2,1)S(1)}, u32[]{:S(2)}) copy-start(bf16[608,384]{1,0:T(8,128)(2,1)S(1)} %collective-permute-done.13.refs_16_.refs_18_) | copy-start | bytes 1400836
  51.5 1.9 %collective-permute-start.14 = (bf16[64,2560]{1,0:T(8,128)(2,1)}, bf16[64,2560]{1,0:T(8,128)(2,1)S(1)}, u32[]{:S(2)}, u32[]{:S(2)}) collective-permute-start(bf16[64,2560]{1,0:T(8,128)(2,1)} %collective-permute-done.9.refs_9_), channel_id=1, source_target_pairs={{0,1},{1,0},{2,3},{3,2},{4,5},{5,4},{6,7},{7,6},{8,9},{9,8},{10,11... | collective-permute-start | bytes 983048 | tf_op jit(solution)/shard_map/ppermute | solution.py:568
  51.6 3.0 %collective-permute-start.3 = (bf16[64,2560]{1,0:T(8,128)(2,1)S(1)}, bf16[64,2560]{1,0:T(8,128)(2,1)S(1)}, u32[]{:S(2)}, u32[]{:S(2)}) collective-permute-start(bf16[64,2560]{1,0:T(8,128)(2,1)S(1)} %collective-permute-done.2.previous.refs_1_), channel_id=1, source_target_pairs={{0,1},{1,0},{2,3},{3,2},{4,5},{5,4},{6,7},{7,6},{8,9},{9,8},{10,11... | collective-permute-start | bytes 983048 | tf_op jit(solution)/shard_map/ppermute | solution.py:568
  52.1 3.2 %collective-permute-start.5 = (bf16[64,2560]{1,0:T(8,128)(2,1)S(1)}, bf16[64,2560]{1,0:T(8,128)(2,1)}, u32[]{:S(2)}, u32[]{:S(2)}) collective-permute-start(bf16[64,2560]{1,0:T(8,128)(2,1)S(1)} %collective-permute-done.4.following.refs_3_), channel_id=1, source_target_pairs={{0,1},{1,0},{2,3},{3,2},{4,5},{5,4},{6,7},{7,6},{8,9},{9,8},{10,11... | collective-permute-start | bytes 983048 | tf_op jit(solution)/shard_map/ppermute | solution.py:568
  52.2 3.1 %copy-start.24 = (bf16[32,2560]{1,0:T(8,128)(2,1)}, bf16[32,2560]{1,0:T(8,128)(2,1)S(1)}, u32[]{:S(2)}) copy-start(bf16[32,2560]{1,0:T(8,128)(2,1)S(1)} %collective-permute-done.17.refs_8_) | copy-start | bytes 491524
  52.2 12.3 %collective-permute-start.18 = (bf16[64,2560]{1,0:T(8,128)(2,1)}, bf16[64,2560]{1,0:T(8,128)(2,1)S(1)}, u32[]{:S(2)}, u32[]{:S(2)}) collective-permute-start(bf16[64,2560]{1,0:T(8,128)(2,1)} %collective-permute-done.9.refs_9_), channel_id=1, source_target_pairs={{0,2},{2,6},{6,4},{4,0},{1,3},{3,7},{7,5},{5,1},{8,10},{10,14},{14... | collective-permute-start | bytes 983048 | tf_op jit(solution)/shard_map/ppermute | solution.py:565
  52.5 2.1 %copy-start.19 = (bf16[64,2560]{1,0:T(8,128)(2,1)}, bf16[64,2560]{1,0:T(8,128)(2,1)S(1)}, u32[]{:S(2)}) copy-start(bf16[64,2560]{1,0:T(8,128)(2,1)S(1)} %collective-permute-done.16.refs_12_) | copy-start | bytes 983044
  52.5 2.0 %collective-permute-start.8 = (bf16[32,2560]{1,0:T(8,128)(2,1)}, bf16[32,2560]{1,0:T(8,128)(2,1)S(1)}, u32[]{:S(2)}, u32[]{:S(2)}) collective-permute-start(bf16[32,2560]{1,0:T(8,128)(2,1)} %collective-permute-done.7.refs_5_), channel_id=1, source_target_pairs={{0,1},{1,0},{2,3},{3,2},{4,5},{5,4},{6,7},{7,6},{8,9},{9,8},{10,11... | collective-permute-start | bytes 491528 | tf_op jit(solution)/shard_map/ppermute | solution.py:568
  53.4 11.0 %copy-start.20 = (bf16[64,2560]{1,0:T(8,128)(2,1)}, bf16[64,2560]{1,0:T(8,128)(2,1)S(1)}, u32[]{:S(2)}) copy-start(bf16[64,2560]{1,0:T(8,128)(2,1)S(1)} %collective-permute-done.14.refs_10_) | copy-start | bytes 983044
  54.6 0.7 copy-start.25
  55.2 0.7 copy-start.22
  64.4 0.7 copy-start.21
  64.5 1.7 %collective-permute-start.19 = (bf16[64,2560]{1,0:T(8,128)(2,1)S(1)}, bf16[64,2560]{1,0:T(8,128)(2,1)S(1)}, u32[]{:S(2)}, u32[]{:S(2)}) collective-permute-start(bf16[64,2560]{1,0:T(8,128)(2,1)S(1)} %collective-permute-done.18.refs_13_), channel_id=1, source_target_pairs={{0,1},{1,0},{2,3},{3,2},{4,5},{5,4},{6,7},{7,6},{8,9},{9,8},{10,11... | collective-permute-start | bytes 983048 | tf_op jit(solution)/shard_map/ppermute | solution.py:568
  66.1 0.7 copy-start.23
  66.1 17.2 %collective-permute-start.22 = (bf16[1216,640]{1,0:T(8,128)(2,1)}, bf16[1216,640]{1,0:T(8,128)(2,1)S(1)}, u32[]{:S(2)}, u32[]{:S(2)}) collective-permute-start(bf16[1216,640]{1,0:T(8,128)(2,1)} %get-tuple-element.106.refs_7_), channel_id=1, source_target_pairs={{0,1},{1,0},{2,3},{3,2},{4,5},{5,4},{6,7},{7,6},{8,9},{9,8},{10,11... | collective-permute-start | bytes 4669448 | tf_op jit(solution)/shard_map/ppermute | solution.py:568
  77.9 5.5 %copy-start.5 = (bf16[1216,640]{1,0:T(8,128)(2,1)S(1)}, bf16[1216,640]{1,0:T(8,128)(2,1)}, u32[]{:S(2)}) copy-start(bf16[1216,640]{1,0:T(8,128)(2,1)} %get-tuple-element.85.refs_6_.w_own) | copy-start | bytes 4669444
  77.9 1.9 %collective-permute-start.21 = (bf16[128,1216]{1,0:T(8,128)(2,1)}, bf16[128,1216]{1,0:T(8,128)(2,1)S(1)}, u32[]{:S(2)}, u32[]{:S(2)}) collective-permute-start(bf16[128,1216]{1,0:T(8,128)(2,1)} %get-tuple-element.103), channel_id=1, source_target_pairs={{0,1},{1,0},{2,3},{3,2},{4,5},{5,4},{6,7},{7,6},{8,9},{9,8},{10,11... | collective-permute-start | bytes 933896 | tf_op jit(solution)/shard_map/ppermute | solution.py:568
  78.1 5.2 %collective-permute-start.20 = (bf16[384,640]{1,0:T(8,128)(2,1)}, bf16[384,640]{1,0:T(8,128)(2,1)S(1)}, u32[]{:S(2)}, u32[]{:S(2)}) collective-permute-start(bf16[384,640]{1,0:T(8,128)(2,1)} %get-tuple-element.104.own), channel_id=1, source_target_pairs={{0,1},{1,0},{2,3},{3,2},{4,5},{5,4},{6,7},{7,6},{8,9},{9,8},{10,11... | collective-permute-start | bytes 1474568 | tf_op jit(solution)/shard_map/ppermute | solution.py:568
  81.0 8.0 %collective-permute-start.26 = (bf16[64,1216]{1,0:T(8,128)(2,1)S(1)}, bf16[64,1216]{1,0:T(8,128)(2,1)S(1)}, u32[]{:S(2)}, u32[]{:S(2)}) collective-permute-start(bf16[64,1216]{1,0:T(8,128)(2,1)S(1)} %get-tuple-element.122), channel_id=1, source_target_pairs={{0,2},{2,6},{6,4},{4,0},{1,3},{3,7},{7,5},{5,1},{8,10},{10,14},{14... | collective-permute-start | bytes 466952 | tf_op jit(solution)/shard_map/ppermute | solution.py:565
  82.9 9.3 %collective-permute-start.23 = (bf16[64,1216]{1,0:T(8,128)(2,1)S(1)}, bf16[64,1216]{1,0:T(8,128)(2,1)S(1)}, u32[]{:S(2)}, u32[]{:S(2)}) collective-permute-start(bf16[64,1216]{1,0:T(8,128)(2,1)S(1)} %get-tuple-element.123), channel_id=1, source_target_pairs={{0,2},{2,6},{6,4},{4,0},{1,3},{3,7},{7,5},{5,1},{8,10},{10,14},{14... | collective-permute-start | bytes 466952 | tf_op jit(solution)/shard_map/ppermute | solution.py:565
  83.3 1.0 copy-start.15
  89.0 7.0 %collective-permute-start.27 = (bf16[64,1216]{1,0:T(8,128)(2,1)S(1)}, bf16[64,1216]{1,0:T(8,128)(2,1)S(1)}, u32[]{:S(2)}, u32[]{:S(2)}) collective-permute-start(bf16[64,1216]{1,0:T(8,128)(2,1)S(1)} %add_convert_fusion.2), channel_id=1, source_target_pairs={{0,2},{2,6},{6,4},{4,0},{1,3},{3,7},{7,5},{5,1},{8,10},{10,14},{14... | collective-permute-start | bytes 466952 | tf_op jit(solution)/shard_map/ppermute | solution.py:565
  92.3 16.0 %copy-start.9 = (f32[128,1216]{1,0:T(8,128)S(1)}, f32[128,1216]{1,0:T(8,128)}, u32[]{:S(2)}) copy-start(f32[128,1216]{1,0:T(8,128)} %copy-done.8) | copy-start | bytes 1867780
  92.3 8.1 %collective-permute-start.24 = (bf16[64,1216]{1,0:T(8,128)(2,1)S(1)}, bf16[64,1216]{1,0:T(8,128)(2,1)S(1)}, u32[]{:S(2)}, u32[]{:S(2)}) collective-permute-start(bf16[64,1216]{1,0:T(8,128)(2,1)S(1)} %add_convert_fusion.4), channel_id=1, source_target_pairs={{0,2},{2,6},{6,4},{4,0},{1,3},{3,7},{7,5},{5,1},{8,10},{10,14},{14... | collective-permute-start | bytes 466952 | tf_op jit(solution)/shard_map/ppermute | solution.py:565
  96.0 7.8 %collective-permute-start.28 = (bf16[64,1216]{1,0:T(8,128)(2,1)S(1)}, bf16[64,1216]{1,0:T(8,128)(2,1)S(1)}, u32[]{:S(2)}, u32[]{:S(2)}) collective-permute-start(bf16[64,1216]{1,0:T(8,128)(2,1)S(1)} %add_convert_fusion.1), channel_id=1, source_target_pairs={{0,2},{2,6},{6,4},{4,0},{1,3},{3,7},{7,5},{5,1},{8,10},{10,14},{14... | collective-permute-start | bytes 466952 | tf_op jit(solution)/shard_map/ppermute | solution.py:565
  100.4 6.3 %collective-permute-start.25 = (bf16[64,1216]{1,0:T(8,128)(2,1)S(1)}, bf16[64,1216]{1,0:T(8,128)(2,1)S(1)}, u32[]{:S(2)}, u32[]{:S(2)}) collective-permute-start(bf16[64,1216]{1,0:T(8,128)(2,1)S(1)} %add_convert_fusion.3), channel_id=1, source_target_pairs={{0,2},{2,6},{6,4},{4,0},{1,3},{3,7},{7,5},{5,1},{8,10},{10,14},{14... | collective-permute-start | bytes 466952 | tf_op jit(solution)/shard_map/ppermute | solution.py:565
  106.9 1.3 %collective-permute-start.29 = (f32[128,128]{1,0:T(8,128)S(1)}, f32[128,128]{1,0:T(8,128)S(1)}, u32[]{:S(2)}, u32[]{:S(2)}) collective-permute-start(f32[128,128]{1,0:T(8,128)S(1)} %get-tuple-element.116.sums), channel_id=1, source_target_pairs={{0,1},{1,0},{2,3},{3,2},{4,5},{5,4},{6,7},{7,6},{8,9},{9,8},{10,11... | collective-permute-start | bytes 196616 | tf_op jit(solution)/shard_map/ppermute | solution.py:568
where the time goes:
time: 110 us; the launch traced here: 109 us
  waiting for transfers between devices  39.3 us (36%)
  starting transfers between devices  27.4 us (25%)
  Pallas kernels  26.9 us (24%)
  local copies, waits for them, and re-layouts  10.9 us (10%)
  other arithmetic  3.21 us (3%)
  between operations  1.7 us (2%)
    ppermute x10, waiting for transfers between devices, step(): return lax.ppermute(moving, 'seq', seq_next)  25 us
    pallas_call x1, Pallas kernels, attend_call(): pl.pallas_call(functools.partial(attend_kernel, slots, count, rows, shard...  11 us
    ppermute x3, starting transfers between devices, step_back(): return lax.ppermute(moving, 'seq', [(b, a) for a, b in seq_next])  10.5 us
    pallas_call x1, Pallas kernels, project_call(): pl.pallas_call(functools.partial(project_kernel, slots, count, rows, shar...  8.46 us
    unnamed x52, local copies, waits for them, and re-layouts  7.54 us
    ppermute x10, starting transfers between devices, step(): return lax.ppermute(moving, 'seq', seq_next)  7.5 us
    ppermute x3, waiting for transfers between devices, step_back(): return lax.ppermute(moving, 'seq', [(b, a) for a, b in seq_next])  6.88 us
    ppermute x11, waiting for transfers between devices, other_core(): return lax.ppermute(moving, 'head', swap)  5.44 us
  transfers between devices with their start and end apart: 30, of which 16 were waited for; matrix products, arithmetic and copies ran while one was open for 6% of the time, Pallas kernels for 21%

commit v1 on v0

--- a/solution.py
+++ b/solution.py
@@ -135,56 +135,29 @@
     return jnp.where(core == 0, rows[:, :half], rows[:, half:])
 
 
-def modulate_kernel(core, states, table_rows, extra, out, normed_out, stretch_out, inv_out):
-    widened = states[...].astype(jnp.float32)
-    centered = widened - jnp.mean(widened, axis=-1, keepdims=True)
-    inv_std = lax.rsqrt(jnp.mean(centered * centered, axis=-1, keepdims=True) + 1e-06)
-    normed = centered * inv_std
-    scale = 1.0 + table_rows[1:2, :]
-    rows, width = states.shape
-    out[:, :width] = (normed * scale + table_rows[0:1, :]).astype(jnp.bfloat16)
-    for n in range(2):
-        out[n * rows // 2 : (n + 1) * rows // 2, width:] = extra[...]
-    normed_out[...] = pick_half(core[0], normed)
-    stretch_out[...] = pick_half(core[0], scale)
-    inv_out[...] = jnp.broadcast_to(inv_std, inv_out.shape)
-
-
-def cotangent_kernel(limit, core, adjoint, table_rows, text, extra, previous, following, opposite, out, half_out, base_out):
-    quarter = opposite.shape[0]
-    first = 2 * quarter - opposite.shape[0]
+def cotangent_kernel(limit, core, adjoint, table_rows, text, extra, previous, following, opposite, out, clip_out):
+    first = previous.shape[0] - opposite.shape[0]
     row = 8 * (text.shape[2] // EXTRA)
-    squares = None
-    for terms in (extra[...], previous[...], following[...]):
-        terms = terms.astype(jnp.float32)[row : row + 1, :]
-        squares = terms if squares is None else squares + terms
-    squares = squares + opposite[...].astype(jnp.float32)[row - first : row - first + 1, :]
+    squares = opposite[...].astype(jnp.float32)[row - first : row - first + 1, :]
+    for terms in (extra, previous, following):
+        squares = squares + terms[...].astype(jnp.float32)[row : row + 1, :]
     squares = jnp.sum(squares, axis=1, keepdims=True)
     clip_scale = jnp.minimum(1.0, limit / jnp.sqrt(squares + 1e-06))
-    gating = table_rows[2:3, :]
-    clipped = clip_scale * adjoint[...]
+    half, width = adjoint.shape
+    out[:, :width] = (table_rows[2:3, :] * (clip_scale * adjoint[...])).astype(jnp.bfloat16)
+    out[:, width:] = extra_columns(text_columns(text, 1), half)
+    clip_out[...] = jnp.broadcast_to(clip_scale, clip_out.shape)
+
+
+def cotangent_call(limit, core, adjoint, table_rows, text, extra, previous, following, opposite):
     rows, width = adjoint.shape
     half = rows // 2
-    columns = extra_columns(text_columns(text, 1), half)
-    out[:, :width] = (gating * clipped).astype(jnp.bfloat16)
-    for n in range(2):
-        out[n * half : (n + 1) * half, width:] = columns
-    base_out[...] = pick_half(core[0], clipped)
-    own = adjoint[pl.ds(pl.multiple_of(core[0] * half, 8), half), :]
-    half_out[:, :width] = (gating * (clip_scale * own)).astype(jnp.bfloat16)
-    half_out[:, width:] = columns
-
-
-def cotangent_call(limit, core, adjoint, table_rows, text, extra, previous, following, opposite):
-    rows, width = adjoint.shape
-    bf16 = jnp.bfloat16
     block = width // EXTRA
     whole = lambda one: pl.BlockSpec(one.shape, lambda i, core: (0,) * one.ndim)
     tail = lambda one: pl.BlockSpec((one.shape[0], EXTRA), lambda i, core: (0, block))
     outs = (
-        jax.ShapeDtypeStruct((rows, width + EXTRA), bf16),
-        jax.ShapeDtypeStruct((rows // 2, width + EXTRA), bf16),
-        jax.ShapeDtypeStruct((rows, width // 2), jnp.float32),
+        jax.ShapeDtypeStruct((half, width + EXTRA), jnp.bfloat16),
+        jax.ShapeDtypeStruct((8, EXTRA), jnp.float32),
     )
     return pl.pallas_call(
         functools.partial(cotangent_kernel, limit),
@@ -192,13 +165,37 @@
         grid_spec=pltpu.PrefetchScalarGridSpec(
             num_scalar_prefetch=1,
             grid=(1,),
-            in_specs=[whole(adjoint), whole(table_rows), whole(text), whole(extra)]
+            in_specs=[pl.BlockSpec((half, width), lambda i, core: (core[0], 0))]
+            + [whole(table_rows), whole(text), whole(extra)]
             + [tail(one) for one in (previous, following, opposite)],
             out_specs=tuple(whole(one) for one in outs),
         ),
-        compiler_params=pltpu.CompilerParams(vmem_limit_bytes=SMALL_GRANT),
-        cost_estimate=pl.CostEstimate(flops=4 * rows * width, bytes_accessed=12 * rows * width, transcendentals=0),
+        compiler_params=pltpu.CompilerParams(vmem_limit_bytes=GRANT),
+        cost_estimate=pl.CostEstimate(flops=4 * half * width, bytes_accessed=6 * half * width, transcendentals=0),
     )(core, adjoint, table_rows, text, extra, previous, following, opposite)
+
+
+def own_kernel(
+    core, states, adjoint, table_rows, text, extra, clip, out, cot_out, normed_out, stretch_out, inv_out, base_out
+):
+    rows, width = states.shape
+    half = rows // 2
+    widened = states[...].astype(jnp.float32)
+    centered = widened - jnp.mean(widened, axis=-1, keepdims=True)
+    inv_std = lax.rsqrt(jnp.mean(centered * centered, axis=-1, keepdims=True) + 1e-06)
+    normed = centered * inv_std
+    scale = 1.0 + table_rows[1:2, :]
+    out[:, :width] = (normed * scale + table_rows[0:1, :]).astype(jnp.bfloat16)
+    normed_out[...] = pick_half(core[0], normed)
+    stretch_out[...] = pick_half(core[0], scale)
+    inv_out[...] = jnp.broadcast_to(inv_std, inv_out.shape)
+    clipped = clip[0:1, 0:1] * adjoint[...]
+    cot_out[:, :width] = (table_rows[2:3, :] * clipped).astype(jnp.bfloat16)
+    base_out[...] = pick_half(core[0], clipped)
+    columns = extra_columns(text_columns(text, 1), half)
+    for n in range(2):
+        out[n * half : (n + 1) * half, width:] = extra[...]
+        cot_out[n * half : (n + 1) * half, width:] = columns
 
 
 class Copies:
@@ -511,14 +508,14 @@
     out[...] = rows.T
 
 
-def local_call(kernel, shapes, scalar_count, *operands):
+def local_call(kernel, shapes, scalar_count, *operands, grant=SMALL_GRANT):
     vmem = spec(pltpu.VMEM)
     return pl.pallas_call(
         kernel,
         out_shape=tuple(jax.ShapeDtypeStruct(*one) for one in shapes),
         in_specs=[spec(pltpu.SMEM)] * scalar_count + [vmem] * (len(operands) - scalar_count),
         out_specs=(vmem,) * len(shapes),
-        compiler_params=pltpu.CompilerParams(vmem_limit_bytes=SMALL_GRANT),
+        compiler_params=pltpu.CompilerParams(vmem_limit_bytes=grant),
         cost_estimate=pl.CostEstimate(
             flops=sum(one.size for one in operands),
             bytes_accessed=sum(one.size * one.dtype.itemsize for one in operands),
@@ -596,24 +593,29 @@
     mod_far = pass_on(mod_near)
     clip_limit = 0.5 * (tok_count * seq_count * model_width) ** 0.5
     extra, *w_first = pin((extra, *w_first))
-    cotangent, cot_half, base = cotangent_call(
+    cot_half, clip = cotangent_call(
         clip_limit, scalars, adjoint_rows, table_rows, text_kv[0], extra, *mod_near, mod_far[1]
     )
     cot_half, mod_far[0] = pin((cot_half, mod_far[0]))
     cot_near = spread(cot_half)
-    modulated, normed_share, scale_share, inv_std = local_call(
-        modulate_kernel,
-        [
-            ((tok_count, model_width + EXTRA), bf16),
+    modulated, cotangent, normed_share, scale_share, inv_std, base = local_call(
+        own_kernel,
+        [((tok_count, model_width + EXTRA), bf16)] * 2
+        + [
             ((tok_count, half_width), f32),
             ((1, half_width), f32),
             ((tok_count, 128), f32),
+            ((tok_count, half_width), f32),
         ],
         1,
         core[None],
         hidden_state,
+        adjoint_rows,
         table_rows,
+        text_kv[0],
         extra,
+        clip,
+        grant=GRANT,
     )
     def pieces(own, received):
         return [own] + [one for moved in received for one in (moved, other_core(moved))]

time: 110 us -> 110 us (level)
  Pallas kernels: 26.9 us -> 31.9 us
  local copies, waits for them, and re-layouts: 10.9 us -> 7.5 us
  starting transfers between devices: 27.4 us -> 25.5 us
    unnamed x52 -> x50, local copies, waits for them, and re-layouts: 7.54 us -> 3.59 us
    pallas_call x3, Pallas kernels: 1.99 us -> 5.12 us  [local_call(): pl.pallas_call(kernel, out_shape=tuple((jax.ShapeDtypeStruct(*one) for on...]
    ppermute x2, waiting for transfers between devices: 1.85 us -> 0.01 us  [shards_by_head(): w_first = [lax.ppermute(part, ('dp', 'head'), first_way) for part in own_w]]
    pallas_call x1, Pallas kernels: 0.95 us -> 2.74 us  [cotangent_call(): pl.pallas_call(functools.partial(cotangent_kernel, limit), out_shape=outs...]
    ppermute x10, starting transfers between devices: 7.5 us -> 5.96 us  [step(): return lax.ppermute(moving, 'seq', seq_next)]
    ppermute x3, waiting for transfers between devices: 6.88 us -> 8.36 us  [step_back(): return lax.ppermute(moving, 'seq', [(b, a) for a, b in seq_next])]
    ppermute x10, waiting for transfers between devices: 25 us -> 26.2 us  [step(): return lax.ppermute(moving, 'seq', seq_next)]
  transfers between devices with their start and end apart: 30 -> 30, of which waited for: 16 -> 16; matrix products, arithmetic and copies ran while one was open for 6% -> 6% of each run, Pallas kernels for 21% -> 25%
where the time goes in v1:
time: 110 us; the launch traced here: 109 us
  waiting for transfers between devices  40.2 us (37%)
  Pallas kernels  31.9 us (29%)
  starting transfers between devices  25.5 us (23%)
  local copies, waits for them, and re-layouts  7.5 us (7%)
  other arithmetic  2.39 us (2%)
  between operations  1.71 us (2%)
    ppermute x10, waiting for transfers between devices, step(): return lax.ppermute(moving, 'seq', seq_next)  26.2 us
    pallas_call x1, Pallas kernels, attend_call(): pl.pallas_call(functools.partial(attend_kernel, slots, count, rows, shard...  11 us
    ppermute x3, starting transfers between devices, step_back(): return lax.ppermute(moving, 'seq', [(b, a) for a, b in seq_next])  9.59 us
    pallas_call x1, Pallas kernels, project_call(): pl.pallas_call(functools.partial(project_kernel, slots, count, rows, shar...  8.49 us
    ppermute x3, waiting for transfers between devices, step_back(): return lax.ppermute(moving, 'seq', [(b, a) for a, b in seq_next])  8.36 us
    ppermute x10, starting transfers between devices, step(): return lax.ppermute(moving, 'seq', seq_next)  5.96 us
    ppermute x11, waiting for transfers between devices, other_core(): return lax.ppermute(moving, 'head', swap)  5.59 us
    pallas_call x3, Pallas kernels, local_call(): pl.pallas_call(kernel, out_shape=tuple((jax.ShapeDtypeStruct(*one) for on...  5.12 us
  transfers between devices with their start and end apart: 30, of which 16 were waited for; matrix products, arithmetic and copies ran while one was open for 6% of the time, Pallas kernels for 25%

profile of v1, /device:TPU:0, one launch (start us, length us, event | category | flops | bytes accessed | tf_op | source)
XLA Modules:
  0.0 109.2 jit_solution(13187770017493618904)
XLA Ops:
  0.7 2.8 %shard_map.91 = (bf16[64,2560]{1,0:T(8,128)(2,1)}, f32[8,2432]{1,0:T(8,128)}, bf16[64,128]{1,0:T(8,128)(2,1)}) custom-call(s32[1]{0:T(128)S(6)} %copy.11.step, s32[1]{0:T(128)} %bitcast.core, bf16[128,2432]{1,0:T(8,128)(2,1)} %bitcast.31, f32[3,28,2432]{2,1,0:T(8,128)} %bitcast.33, f32[128,2432]{1,0:T(8,128)} %bitcast.28, bf16[8,2,640]{2,1,0:T(2,128)(2,1)} %bitcast.34), custom_call_target="tpu_custom_call" | custom-call | flops 1245184 | bytes 2490368 | tf_op jit(solution)/shard_map/pallas_call | solution.py:110
  3.6 4.0 %collective-permute-start.3 = (bf16[64,2560]{1,0:T(8,128)(2,1)}, bf16[64,2560]{1,0:T(8,128)(2,1)S(1)}, u32[]{:S(2)}, u32[]{:S(2)}) collective-permute-start(bf16[64,2560]{1,0:T(8,128)(2,1)} %get-tuple-element.65), channel_id=1, source_target_pairs={{2,0},{6,2},{4,6},{0,4},{3,1},{7,3},{5,7},{1,5},{10,8},{14,10},{12... | collective-permute-start | bytes 983048 | tf_op jit(solution)/shard_map/ppermute | solution.py:568
  7.6 1.7 %dynamic-slice_bitcast_fusion.1 = (bf16[608,192]{1,0:T(8,128)(2,1)S(1)}, bf16[608,192]{1,0:T(8,128)(2,1)S(1)}, bf16[608,192]{1,0:T(8,128)(2,1)S(1)}) fusion(bf16[608,3,640]{2,0,1:T(8,128)(2,1)} %param.15, s32[]{:T(128)S(6)} %select_n.103), kind=kLoop, calls=%fused_computation.8 | loop fusion | bytes 1400836 | tf_op jit(solution)/shard_map/squeeze | solution.py:584
  9.3 0.2 dynamic-slice_bitcast_fusion
  9.5 0.2 pad_maximum_fusion.1.refs_13_.refs_15_
  9.7 1.6 %collective-permute-start.1 = (bf16[608,384]{1,0:T(8,128)(2,1)S(1)}, bf16[608,384]{1,0:T(8,128)(2,1)S(1)}, u32[]{:S(2)}, u32[]{:S(2)}) collective-permute-start(bf16[608,384]{1,0:T(8,128)(2,1)S(1)} %pad_maximum_fusion.1.refs_13_.refs_15_), channel_id=1, source_target_pairs={{0,8},{1,17},{8,0},{9,25},{16,24},{17,1},{24,16},{25,9},{2,10},{3,... | collective-permute-start | bytes 1400840 | tf_op jit(solution)/shard_map/ppermute | solution.py:589
  11.2 0.9 pad_maximum_fusion.refs_9_
  12.2 0.5 collective-permute-start
  12.7 1.5 %collective-permute-start.11 = (bf16[608,384]{1,0:T(8,128)(2,1)S(1)}, bf16[608,384]{1,0:T(8,128)(2,1)S(1)}, u32[]{:S(2)}, u32[]{:S(2)}) collective-permute-start(bf16[608,384]{1,0:T(8,128)(2,1)S(1)} %pad_maximum_fusion.1.refs_13_.refs_15_), channel_id=1, source_target_pairs={{0,16},{1,9},{8,24},{9,1},{16,0},{17,25},{24,8},{25,17},{2,18},{3,... | collective-permute-start | bytes 1400840 | tf_op jit(solution)/shard_map/ppermute | solution.py:590
  14.2 1.9 %collective-permute-done.3.following.refs_3_ = bf16[64,2560]{1,0:T(8,128)(2,1)S(1)} collective-permute-done((bf16[64,2560]{1,0:T(8,128)(2,1)}, bf16[64,2560]{1,0:T(8,128)(2,1)S(1)}, u32[]{:S(2)}, u32[]{:S(2)}) %collective-permute-start.3) | collective-permute-done | bytes 327712 | tf_op jit(solution)/shard_map/ppermute | solution.py:568
  16.1 0.7 slice.16
  16.8 3.3 %collective-permute-start.4 = (bf16[32,2560]{1,0:T(8,128)(2,1)}, bf16[32,2560]{1,0:T(8,128)(2,1)S(1)}, u32[]{:S(2)}, u32[]{:S(2)}) collective-permute-start(bf16[32,2560]{1,0:T(8,128)(2,1)} %slice.16), channel_id=1, source_target_pairs={{2,0},{6,2},{4,6},{0,4},{3,1},{7,3},{5,7},{1,5},{10,8},{14,10},{12... | collective-permute-start | bytes 491528 | tf_op jit(solution)/shard_map/ppermute | solution.py:568
  20.1 4.7 %collective-permute-done.2.previous.refs_1_ = bf16[64,2560]{1,0:T(8,128)(2,1)S(1)} collective-permute-done((bf16[64,2560]{1,0:T(8,128)(2,1)}, bf16[64,2560]{1,0:T(8,128)(2,1)S(1)}, u32[]{:S(2)}, u32[]{:S(2)}) %collective-permute-start.2) | collective-permute-done | bytes 327712 | tf_op jit(solution)/shard_map/ppermute | solution.py:562
  24.8 0.7 slice.17
  25.5 0.7 collective-permute-start.7
  26.2 1.5 %collective-permute-start.10 = (bf16[608,384]{1,0:T(8,128)(2,1)}, bf16[608,384]{1,0:T(8,128)(2,1)}, u32[]{:S(2)}, u32[]{:S(2)}) collective-permute-start(bf16[608,384]{1,0:T(8,128)(2,1)} %pad_maximum_fusion.refs_9_), channel_id=1, source_target_pairs={{0,16},{1,9},{8,24},{9,1},{16,0},{17,25},{24,8},{25,17},{2,18},{3,... | collective-permute-start | bytes 1400840 | tf_op jit(solution)/shard_map/ppermute | solution.py:590
  28.4 0.6 stack.67.core.scalars
  29.1 0.7 copy-done.14
  29.7 2.7 %shard_map.92 = (bf16[64,2560]{1,0:T(8,128)(2,1)}, f32[8,128]{1,0:T(8,128)}) custom-call(s32[14]{0:T(128)} %stack.67.core.scalars, f32[128,2432]{1,0:T(8,128)} %bitcast.29, f32[8,2432]{1,0:T(8,128)} %get-tuple-element.63.table_rows, bf16[8,2,640]{2,1,0:T(2,128)(2,1)} %bitcast.35, bf16[64,128]{1,0:T(8,128)(2,1)} %get-tuple-element.68.extra, ...), custom_call_target="tpu_custom_call" | custom-call | flops 622592 | bytes 933888 | tf_op jit(solution)/shard_map/pallas_call | solution.py:162
  32.5 0.3 collective-permute-done.7.refs_5_
  32.8 2.3 %collective-permute-start.15 = (bf16[64,2560]{1,0:T(8,128)(2,1)}, bf16[64,2560]{1,0:T(8,128)(2,1)}, u32[]{:S(2)}, u32[]{:S(2)}) collective-permute-start(bf16[64,2560]{1,0:T(8,128)(2,1)} %get-tuple-element.76), channel_id=1, source_target_pairs={{2,0},{6,2},{4,6},{0,4},{3,1},{7,3},{5,7},{1,5},{10,8},{14,10},{12... | collective-permute-start | bytes 983048 | tf_op jit(solution)/shard_map/ppermute | solution.py:568
  35.0 1.5 %collective-permute-start.12 = (bf16[608,384]{1,0:T(8,128)(2,1)S(1)}, bf16[608,384]{1,0:T(8,128)(2,1)S(1)}, u32[]{:S(2)}, u32[]{:S(2)}) collective-permute-start(bf16[608,384]{1,0:T(8,128)(2,1)S(1)} %collective-permute-done.refs_10_), channel_id=1, source_target_pairs={{0,16},{1,9},{8,24},{9,1},{16,0},{17,25},{24,8},{25,17},{2,18},{3,... | collective-permute-start | bytes 1400840 | tf_op jit(solution)/shard_map/ppermute | solution.py:625
  36.5 0.5 collective-permute-start.13
  37.1 6.5 %collective-permute-done.15.refs_11_ = bf16[64,2560]{1,0:T(8,128)(2,1)} collective-permute-done((bf16[64,2560]{1,0:T(8,128)(2,1)}, bf16[64,2560]{1,0:T(8,128)(2,1)}, u32[]{:S(2)}, u32[]{:S(2)}) %collective-permute-start.15) | collective-permute-done | bytes 327712 | tf_op jit(solution)/shard_map/ppermute | solution.py:568
  43.6 3.7 %shard_map.93 = (bf16[128,2560]{1,0:T(8,128)(2,1)}, bf16[128,2560]{1,0:T(8,128)(2,1)}, f32[128,1216]{1,0:T(8,128)}, f32[1,1216]{1,0:T(1,128)}, f32[128,128]{1,0:T(8,128)}, /*index=5*/f32[128,1216]{1,0:T(8,128)}) custom-call(s32[1]{0:T(128)} %bitcast.core, bf16[128,2432]{1,0:T(8,128)(2,1)} %bitcast.32, f32[128,2432]{1,0:T(8,128)} %bitcast.30, ...), custom_call_target="tpu_custom_call" | custom-call | flops 661505 | bytes 1986564 | tf_op jit(solution)/shard_map/pallas_call | solution.py:513
  47.3 0.6 collective-permute-start.17
  47.9 3.6 %collective-permute-done.9.refs_9_ = bf16[64,2560]{1,0:T(8,128)(2,1)S(1)} collective-permute-done((bf16[64,2560]{1,0:T(8,128)(2,1)}, bf16[64,2560]{1,0:T(8,128)(2,1)S(1)}, u32[]{:S(2)}, u32[]{:S(2)}) %collective-permute-start.9) | collective-permute-done | bytes 327712 | tf_op jit(solution)/shard_map/ppermute | solution.py:562
  51.4 0.1 collective-permute-start.14
  51.5 0.5 collective-permute-start.5
  52.0 0.1 collective-permute-start.6
  52.1 0.2 collective-permute-start.18
  52.3 0.3 collective-permute-start.8
  52.6 0.5 collective-permute-done.14.refs_10_
  53.1 1.1 %collective-permute-done.8.refs_6_ = bf16[32,2560]{1,0:T(8,128)(2,1)S(1)} collective-permute-done((bf16[32,2560]{1,0:T(8,128)(2,1)}, bf16[32,2560]{1,0:T(8,128)(2,1)S(1)}, u32[]{:S(2)}, u32[]{:S(2)}) %collective-permute-start.8) | collective-permute-done | bytes 163872 | tf_op jit(solution)/shard_map/ppermute | solution.py:565
  54.3 0.7 copy-done.24
  55.0 0.7 copy-done.21
  55.7 8.5 %shard_map.94 = (bf16[512,576]{1,0:T(8,128)(2,1)}, bf16[192,512]{1,0:T(8,128)(2,1)}, f32[512,384]{1,0:T(8,128)}, f32[512,384]{1,0:T(8,128)}, bf16[3,32,64]{2,1,0...) custom-call(s32[14]{0:T(128)} %stack.67.core.scalars, ...), custom_call_target="tpu_custom_call" | custom-call | flops 1434451968 | bytes 7798784 | tf_op jit(solution)/shard_map/pallas_call | solution.py:410
  64.2 0.3 collective-permute-start.19
  64.6 1.3 %collective-permute-done.19.refs_14_ = bf16[64,2560]{1,0:T(8,128)(2,1)S(1)} collective-permute-done((bf16[64,2560]{1,0:T(8,128)(2,1)S(1)}, bf16[64,2560]{1,0:T(8,128)(2,1)S(1)}, u32[]{:S(2)}, u32[]{:S(2)}) %collective-permute-start.19) | collective-permute-done | bytes 327712 | tf_op jit(solution)/shard_map/ppermute | solution.py:565
  65.9 0.3 collective-permute-start.22
  66.2 0.4 copy-done.22
  66.6 11.0 %shard_map.95 = (f32[128,1216]{1,0:T(8,128)}, bf16[128,1216]{1,0:T(8,128)(2,1)}, bf16[384,640]{1,0:T(8,128)(2,1)}) custom-call(s32[14]{0:T(128)} %stack.67.core.scalars, f32[2,64]{1,0:T(2,128)} %gain.3, bf16[512,576]{1,0:T(8,128)(2,1)} %get-tuple-element.81.refs_0_, bf16[192,512]{1,0:T(8,128)(2,1)} %get-tuple-element.82.refs_1_, ...), custom_call_target="tpu_custom_call" | custom-call | flops 981467136 | bytes 4358144 | tf_op jit(solution)/shard_map/pallas_call | solution.py:441
  77.7 0.3 collective-permute-start.21
  78.0 0.2 collective-permute-start.20
  78.3 1.3 %collective-permute-done.21 = bf16[128,1216]{1,0:T(8,128)(2,1)S(1)} collective-permute-done((bf16[128,1216]{1,0:T(8,128)(2,1)}, bf16[128,1216]{1,0:T(8,128)(2,1)S(1)}, u32[]{:S(2)}, u32[]{:S(2)}) %collective-permute-start.21) | collective-permute-done | bytes 311328 | tf_op jit(solution)/shard_map/ppermute | solution.py:565
  79.6 1.2 %add_convert_fusion = bf16[128,1216]{1,0:T(8,128)(2,1)S(1)} fusion(f32[128,1216]{1,0:T(8,128)} %get-tuple-element.104, bf16[128,1216]{1,0:T(8,128)(2,1)S(1)} %collective-permute-done.21), kind=kLoop, calls=%fused_computation | loop fusion | flops 466944 | bytes 1245184 | tf_op jit(solution)/shard_map/convert_element_type | solution.py:642
  80.8 1.6 %collective-permute-start.26 = (bf16[64,1216]{1,0:T(8,128)(2,1)S(1)}, bf16[64,1216]{1,0:T(8,128)(2,1)S(1)}, u32[]{:S(2)}, u32[]{:S(2)}) collective-permute-start(bf16[64,1216]{1,0:T(8,128)(2,1)S(1)} %get-tuple-element.124), channel_id=1, source_target_pairs={{0,2},{2,6},{6,4},{4,0},{1,3},{3,7},{7,5},{5,1},{8,10},{10,14},{14... | collective-permute-start | bytes 466952 | tf_op jit(solution)/shard_map/ppermute | solution.py:562
  82.4 0.7 collective-permute-start.23
  83.1 1.0 copy-done.6
  84.1 1.7 %shard_map.96 = (f32[64,1216]{1,0:T(8,128)S(1)}, f32[64,1216]{1,0:T(8,128)S(1)}, f32[64,1216]{1,0:T(8,128)S(1)}, f32[64,1216]{1,0:T(8,128)S(1)}, f32[64,1216]{1,0:T(8,128)S(1)}, /*index=5*/f32[64,1216]{1,0:T(8,128)S(1)}) custom-call(bf16[384,640]{1,0:T(8,128)(2,1)S(1)} %copy-done.6, bf16[384,640]{1,0:T(8,128)(2,1)S(1)} %collective-permute-done.20.other, ...), custom_call_target="tpu_custom_call" | custom-call | flops 1195376640 | bytes 5963776 | tf_op jit(solution)/shard_map/pallas_call | solution.py:477
  85.8 2.9 %collective-permute-done.26 = bf16[64,1216]{1,0:T(8,128)(2,1)S(1)} collective-permute-done((bf16[64,1216]{1,0:T(8,128)(2,1)S(1)}, bf16[64,1216]{1,0:T(8,128)(2,1)S(1)}, u32[]{:S(2)}, u32[]{:S(2)}) %collective-permute-start.26) | collective-permute-done | bytes 155680 | tf_op jit(solution)/shard_map/ppermute | solution.py:562
  88.8 0.7 collective-permute-start.27
  89.5 2.5 %collective-permute-done.23 = bf16[64,1216]{1,0:T(8,128)(2,1)S(1)} collective-permute-done((bf16[64,1216]{1,0:T(8,128)(2,1)S(1)}, bf16[64,1216]{1,0:T(8,128)(2,1)S(1)}, u32[]{:S(2)}, u32[]{:S(2)}) %collective-permute-start.23) | collective-permute-done | bytes 155680 | tf_op jit(solution)/shard_map/ppermute | solution.py:562
  92.1 0.9 collective-permute-start.24
  93.0 2.5 %collective-permute-done.27 = bf16[64,1216]{1,0:T(8,128)(2,1)S(1)} collective-permute-done((bf16[64,1216]{1,0:T(8,128)(2,1)S(1)}, bf16[64,1216]{1,0:T(8,128)(2,1)S(1)}, u32[]{:S(2)}, u32[]{:S(2)}) %collective-permute-start.27) | collective-permute-done | bytes 155680 | tf_op jit(solution)/shard_map/ppermute | solution.py:562
  95.6 1.1 %collective-permute-start.28 = (bf16[64,1216]{1,0:T(8,128)(2,1)S(1)}, bf16[64,1216]{1,0:T(8,128)(2,1)S(1)}, u32[]{:S(2)}, u32[]{:S(2)}) collective-permute-start(bf16[64,1216]{1,0:T(8,128)(2,1)S(1)} %add_convert_fusion.1), channel_id=1, source_target_pairs={{0,2},{2,6},{6,4},{4,0},{1,3},{3,7},{7,5},{5,1},{8,10},{10,14},{14... | collective-permute-start | bytes 466952 | tf_op jit(solution)/shard_map/ppermute | solution.py:562
  96.7 3.5 %collective-permute-done.24 = bf16[64,1216]{1,0:T(8,128)(2,1)S(1)} collective-permute-done((bf16[64,1216]{1,0:T(8,128)(2,1)S(1)}, bf16[64,1216]{1,0:T(8,128)(2,1)S(1)}, u32[]{:S(2)}, u32[]{:S(2)}) %collective-permute-start.24) | collective-permute-done | bytes 155680 | tf_op jit(solution)/shard_map/ppermute | solution.py:562
  100.2 0.1 collective-permute-start.25
  100.3 3.2 %collective-permute-done.28.far = bf16[64,1216]{1,0:T(8,128)(2,1)S(1)} collective-permute-done((bf16[64,1216]{1,0:T(8,128)(2,1)S(1)}, bf16[64,1216]{1,0:T(8,128)(2,1)S(1)}, u32[]{:S(2)}, u32[]{:S(2)}) %collective-permute-start.28) | collective-permute-done | bytes 155680 | tf_op jit(solution)/shard_map/ppermute | solution.py:562
  103.4 3.0 %collective-permute-done.25.near = bf16[64,1216]{1,0:T(8,128)(2,1)S(1)} collective-permute-done((bf16[64,1216]{1,0:T(8,128)(2,1)S(1)}, bf16[64,1216]{1,0:T(8,128)(2,1)S(1)}, u32[]{:S(2)}, u32[]{:S(2)}) %collective-permute-start.25) | collective-permute-done | bytes 155680 | tf_op jit(solution)/shard_map/ppermute | solution.py:562
  106.5 0.2 shard_map.97
  106.7 0.1 collective-permute-start.29
  106.8 1.2 %collective-permute-done.29.other = f32[128,128]{1,0:T(8,128)S(1)} collective-permute-done((f32[128,128]{1,0:T(8,128)S(1)}, f32[128,128]{1,0:T(8,128)S(1)}, u32[]{:S(2)}, u32[]{:S(2)}) %collective-permute-start.29) | collective-permute-done | bytes 65568 | tf_op jit(solution)/shard_map/ppermute | solution.py:565
  108.0 1.2 %shard_map.98 = f32[1216,128]{1,0:T(8,128)} custom-call(f32[128,1216]{1,0:T(8,128)S(1)} %get-tuple-element.117.grad, f32[128,128]{1,0:T(8,128)S(1)} %get-tuple-element.118.sums, f32[128,128]{1,0:T(8,128)S(1)} %collective-permute-done.29.other, f32[128,1216]{1,0:T(8,128)S(1)} %copy-done.1, f32[128,1216]{1,0:T(8,128)S(1)} %copy-done.3, f32[128,128]{1,0:T(8,128)S(1)} %copy-done.4), custom_call_target="tpu_custom_call" | custom-call | flops 516096 | bytes 2064384 | tf_op jit(solution)/shard_map/pallas_call | solution.py:513
  (67 shorter events, 0.3 us)
Async XLA Ops:
  0.0 9.3 %copy-start = (bf16[640,608]{0,1:T(8,128)(2,1)S(1)}, bf16[640,608]{0,1:T(8,128)(2,1)}, u32[]{:S(2)}) copy-start(bf16[640,608]{0,1:T(8,128)(2,1)} %param.17) | copy-start | bytes 2334724
  3.6 12.5 %collective-permute-start.3 = (bf16[64,2560]{1,0:T(8,128)(2,1)}, bf16[64,2560]{1,0:T(8,128)(2,1)S(1)}, u32[]{:S(2)}, u32[]{:S(2)}) collective-permute-start(bf16[64,2560]{1,0:T(8,128)(2,1)} %get-tuple-element.65), channel_id=1, source_target_pairs={{2,0},{6,2},{4,6},{0,4},{3,1},{7,3},{5,7},{1,5},{10,8},{14,10},{12... | collective-permute-start | bytes 983048 | tf_op jit(solution)/shard_map/ppermute | solution.py:568
  7.6 17.2 %collective-permute-start.2 = (bf16[64,2560]{1,0:T(8,128)(2,1)}, bf16[64,2560]{1,0:T(8,128)(2,1)S(1)}, u32[]{:S(2)}, u32[]{:S(2)}) collective-permute-start(bf16[64,2560]{1,0:T(8,128)(2,1)} %get-tuple-element.65), channel_id=1, source_target_pairs={{0,2},{2,6},{6,4},{4,0},{1,3},{3,7},{7,5},{5,1},{8,10},{10,14},{14... | collective-permute-start | bytes 983048 | tf_op jit(solution)/shard_map/ppermute | solution.py:562
  9.7 22.8 %copy-start.7 = (bf16[608,384]{1,0:T(8,128)(2,1)}, bf16[608,384]{1,0:T(8,128)(2,1)S(1)}, u32[]{:S(2)}) copy-start(bf16[608,384]{1,0:T(8,128)(2,1)S(1)} %pad_maximum_fusion.1.refs_13_.refs_15_) | copy-start | bytes 1400836
  9.7 16.5 %collective-permute-start.1 = (bf16[608,384]{1,0:T(8,128)(2,1)S(1)}, bf16[608,384]{1,0:T(8,128)(2,1)S(1)}, u32[]{:S(2)}, u32[]{:S(2)}) collective-permute-start(bf16[608,384]{1,0:T(8,128)(2,1)S(1)} %pad_maximum_fusion.1.refs_13_.refs_15_), channel_id=1, source_target_pairs={{0,8},{1,17},{8,0},{9,25},{16,24},{17,1},{24,16},{25,9},{2,10},{3,... | collective-permute-start | bytes 1400840 | tf_op jit(solution)/shard_map/ppermute | solution.py:589
  12.2 16.9 %collective-permute-start = (bf16[608,384]{1,0:T(8,128)(2,1)}, bf16[608,384]{1,0:T(8,128)(2,1)S(1)}, u32[]{:S(2)}, u32[]{:S(2)}) collective-permute-start(bf16[608,384]{1,0:T(8,128)(2,1)} %pad_maximum_fusion.refs_9_), channel_id=1, source_target_pairs={{0,8},{1,17},{8,0},{9,25},{16,24},{17,1},{24,16},{25,9},{2,10},{3,... | collective-permute-start | bytes 1400840 | tf_op jit(solution)/shard_map/ppermute | solution.py:589
  12.7 24.4 %collective-permute-start.11 = (bf16[608,384]{1,0:T(8,128)(2,1)S(1)}, bf16[608,384]{1,0:T(8,128)(2,1)S(1)}, u32[]{:S(2)}, u32[]{:S(2)}) collective-permute-start(bf16[608,384]{1,0:T(8,128)(2,1)S(1)} %pad_maximum_fusion.1.refs_13_.refs_15_), channel_id=1, source_target_pairs={{0,16},{1,9},{8,24},{9,1},{16,0},{17,25},{24,8},{25,17},{2,18},{3,... | collective-permute-start | bytes 1400840 | tf_op jit(solution)/shard_map/ppermute | solution.py:590
  16.1 12.9 %copy-start.8 = (bf16[64,2560]{1,0:T(8,128)(2,1)}, bf16[64,2560]{1,0:T(8,128)(2,1)S(1)}, u32[]{:S(2)}) copy-start(bf16[64,2560]{1,0:T(8,128)(2,1)S(1)} %collective-permute-done.3.following.refs_3_) | copy-start | bytes 983044
  16.8 12.2 %collective-permute-start.4 = (bf16[32,2560]{1,0:T(8,128)(2,1)}, bf16[32,2560]{1,0:T(8,128)(2,1)S(1)}, u32[]{:S(2)}, u32[]{:S(2)}) collective-permute-start(bf16[32,2560]{1,0:T(8,128)(2,1)} %slice.16), channel_id=1, source_target_pairs={{2,0},{6,2},{4,6},{0,4},{3,1},{7,3},{5,7},{1,5},{10,8},{14,10},{12... | collective-permute-start | bytes 491528 | tf_op jit(solution)/shard_map/ppermute | solution.py:568
  24.8 4.2 %copy-start.10 = (bf16[64,2560]{1,0:T(8,128)(2,1)}, bf16[64,2560]{1,0:T(8,128)(2,1)S(1)}, u32[]{:S(2)}) copy-start(bf16[64,2560]{1,0:T(8,128)(2,1)S(1)} %collective-permute-done.2.previous.refs_1_) | copy-start | bytes 983044
  25.5 7.2 %collective-permute-start.7 = (bf16[32,2560]{1,0:T(8,128)(2,1)}, bf16[32,2560]{1,0:T(8,128)(2,1)}, u32[]{:S(2)}, u32[]{:S(2)}) collective-permute-start(bf16[32,2560]{1,0:T(8,128)(2,1)} %slice.17), channel_id=1, source_target_pairs={{0,2},{2,6},{6,4},{4,0},{1,3},{3,7},{7,5},{5,1},{8,10},{10,14},{14... | collective-permute-start | bytes 491528 | tf_op jit(solution)/shard_map/ppermute | solution.py:562
  26.2 21.1 %copy-start.12 = (bf16[608,384]{1,0:T(8,128)(2,1)}, bf16[608,384]{1,0:T(8,128)(2,1)S(1)}, u32[]{:S(2)}) copy-start(bf16[608,384]{1,0:T(8,128)(2,1)S(1)} %collective-permute-done.1.refs_14_.refs_16_) | copy-start | bytes 1400836
  26.2 21.1 %collective-permute-start.10 = (bf16[608,384]{1,0:T(8,128)(2,1)}, bf16[608,384]{1,0:T(8,128)(2,1)}, u32[]{:S(2)}, u32[]{:S(2)}) collective-permute-start(bf16[608,384]{1,0:T(8,128)(2,1)} %pad_maximum_fusion.refs_9_), channel_id=1, source_target_pairs={{0,16},{1,9},{8,24},{9,1},{16,0},{17,25},{24,8},{25,17},{2,18},{3,... | collective-permute-start | bytes 1400840 | tf_op jit(solution)/shard_map/ppermute | solution.py:590
  29.0 26.7 %copy-start.16 = (bf16[608,384]{1,0:T(8,128)(2,1)}, bf16[608,384]{1,0:T(8,128)(2,1)S(1)}, u32[]{:S(2)}) copy-start(bf16[608,384]{1,0:T(8,128)(2,1)S(1)} %collective-permute-done.refs_10_) | copy-start | bytes 1400836
  29.0 0.7 copy-start.14
  32.5 14.8 %copy-start.15 = (bf16[32,2560]{1,0:T(8,128)(2,1)S(1)}, bf16[32,2560]{1,0:T(8,128)(2,1)}, u32[]{:S(2)}) copy-start(bf16[32,2560]{1,0:T(8,128)(2,1)} %copy-done.14) | copy-start | bytes 491524
  32.5 19.1 %copy-start.11 = (bf16[64,2560]{1,0:T(8,128)(2,1)S(1)}, bf16[64,2560]{1,0:T(8,128)(2,1)}, u32[]{:S(2)}) copy-start(bf16[64,2560]{1,0:T(8,128)(2,1)} %copy-done.10) | copy-start | bytes 983044
  32.5 19.5 %copy-start.9 = (bf16[64,2560]{1,0:T(8,128)(2,1)S(1)}, bf16[64,2560]{1,0:T(8,128)(2,1)}, u32[]{:S(2)}) copy-start(bf16[64,2560]{1,0:T(8,128)(2,1)} %copy-done.8) | copy-start | bytes 983044
  32.8 10.8 %collective-permute-start.15 = (bf16[64,2560]{1,0:T(8,128)(2,1)}, bf16[64,2560]{1,0:T(8,128)(2,1)}, u32[]{:S(2)}, u32[]{:S(2)}) collective-permute-start(bf16[64,2560]{1,0:T(8,128)(2,1)} %get-tuple-element.76), channel_id=1, source_target_pairs={{2,0},{6,2},{4,6},{0,4},{3,1},{7,3},{5,7},{1,5},{10,8},{14,10},{12... | collective-permute-start | bytes 983048 | tf_op jit(solution)/shard_map/ppermute | solution.py:568
  35.0 16.4 %collective-permute-start.12 = (bf16[608,384]{1,0:T(8,128)(2,1)S(1)}, bf16[608,384]{1,0:T(8,128)(2,1)S(1)}, u32[]{:S(2)}, u32[]{:S(2)}) collective-permute-start(bf16[608,384]{1,0:T(8,128)(2,1)S(1)} %collective-permute-done.refs_10_), channel_id=1, source_target_pairs={{0,16},{1,9},{8,24},{9,1},{16,0},{17,25},{24,8},{25,17},{2,18},{3,... | collective-permute-start | bytes 1400840 | tf_op jit(solution)/shard_map/ppermute | solution.py:625
  36.5 14.9 %collective-permute-start.13 = (bf16[608,384]{1,0:T(8,128)(2,1)S(1)}, bf16[608,384]{1,0:T(8,128)(2,1)}, u32[]{:S(2)}, u32[]{:S(2)}) collective-permute-start(bf16[608,384]{1,0:T(8,128)(2,1)S(1)} %collective-permute-done.1.refs_14_.refs_16_), channel_id=1, source_target_pairs={{0,16},{1,9},{8,24},{9,1},{16,0},{17,25},{24,8},{25,17},{2,18},{3,... | collective-permute-start | bytes 1400840 | tf_op jit(solution)/shard_map/ppermute | solution.py:625
  37.1 18.6 %copy-start.13 = (bf16[608,384]{1,0:T(8,128)(2,1)}, bf16[608,384]{1,0:T(8,128)(2,1)S(1)}, u32[]{:S(2)}) copy-start(bf16[608,384]{1,0:T(8,128)(2,1)S(1)} %collective-permute-done.11.refs_15_.refs_17_) | copy-start | bytes 1400836
  37.1 14.4 %collective-permute-start.9 = (bf16[64,2560]{1,0:T(8,128)(2,1)}, bf16[64,2560]{1,0:T(8,128)(2,1)S(1)}, u32[]{:S(2)}, u32[]{:S(2)}) collective-permute-start(bf16[64,2560]{1,0:T(8,128)(2,1)} %get-tuple-element.76), channel_id=1, source_target_pairs={{0,2},{2,6},{6,4},{4,0},{1,3},{3,7},{7,5},{5,1},{8,10},{10,14},{14... | collective-permute-start | bytes 983048 | tf_op jit(solution)/shard_map/ppermute | solution.py:562
  43.6 8.7 %collective-permute-start.16 = (bf16[64,2560]{1,0:T(8,128)(2,1)}, bf16[64,2560]{1,0:T(8,128)(2,1)}, u32[]{:S(2)}, u32[]{:S(2)}) collective-permute-start(bf16[64,2560]{1,0:T(8,128)(2,1)} %collective-permute-done.15.refs_11_), channel_id=1, source_target_pairs={{0,1},{1,0},{2,3},{3,2},{4,5},{5,4},{6,7},{7,6},{8,9},{9,8},{10,11... | collective-permute-start | bytes 983048 | tf_op jit(solution)/shard_map/ppermute | solution.py:565
  47.3 4.8 %collective-permute-start.17 = (bf16[32,2560]{1,0:T(8,128)(2,1)S(1)}, bf16[32,2560]{1,0:T(8,128)(2,1)S(1)}, u32[]{:S(2)}, u32[]{:S(2)}) collective-permute-start(bf16[32,2560]{1,0:T(8,128)(2,1)S(1)} %copy-done.15), channel_id=1, source_target_pairs={{0,1},{1,0},{2,3},{3,2},{4,5},{5,4},{6,7},{7,6},{8,9},{9,8},{10,11... | collective-permute-start | bytes 491528 | tf_op jit(solution)/shard_map/ppermute | solution.py:565
  51.4 14.8 %copy-start.18 = (bf16[64,2560]{1,0:T(8,128)(2,1)}, bf16[64,2560]{1,0:T(8,128)(2,1)S(1)}, u32[]{:S(2)}) copy-start(bf16[64,2560]{1,0:T(8,128)(2,1)S(1)} %collective-permute-done.9.refs_9_) | copy-start | bytes 983044
  51.4 4.3 %copy-start.17 = (bf16[608,384]{1,0:T(8,128)(2,1)}, bf16[608,384]{1,0:T(8,128)(2,1)S(1)}, u32[]{:S(2)}) copy-start(bf16[608,384]{1,0:T(8,128)(2,1)S(1)} %collective-permute-done.12.refs_12_) | copy-start | bytes 1400836
  51.4 1.7 %collective-permute-start.14 = (bf16[64,2560]{1,0:T(8,128)(2,1)S(1)}, bf16[64,2560]{1,0:T(8,128)(2,1)S(1)}, u32[]{:S(2)}, u32[]{:S(2)}) collective-permute-start(bf16[64,2560]{1,0:T(8,128)(2,1)S(1)} %collective-permute-done.9.refs_9_), channel_id=1, source_target_pairs={{0,1},{1,0},{2,3},{3,2},{4,5},{5,4},{6,7},{7,6},{8,9},{9,8},{10,11... | collective-permute-start | bytes 983048 | tf_op jit(solution)/shard_map/ppermute | solution.py:565
  51.5 2.8 %collective-permute-start.5 = (bf16[64,2560]{1,0:T(8,128)(2,1)S(1)}, bf16[64,2560]{1,0:T(8,128)(2,1)S(1)}, u32[]{:S(2)}, u32[]{:S(2)}) collective-permute-start(bf16[64,2560]{1,0:T(8,128)(2,1)S(1)} %copy-done.11), channel_id=1, source_target_pairs={{0,1},{1,0},{2,3},{3,2},{4,5},{5,4},{6,7},{7,6},{8,9},{9,8},{10,11... | collective-permute-start | bytes 983048 | tf_op jit(solution)/shard_map/ppermute | solution.py:565
  52.0 3.7 %collective-permute-start.6 = (bf16[64,2560]{1,0:T(8,128)(2,1)S(1)}, bf16[64,2560]{1,0:T(8,128)(2,1)}, u32[]{:S(2)}, u32[]{:S(2)}) collective-permute-start(bf16[64,2560]{1,0:T(8,128)(2,1)S(1)} %copy-done.9), channel_id=1, source_target_pairs={{0,1},{1,0},{2,3},{3,2},{4,5},{5,4},{6,7},{7,6},{8,9},{9,8},{10,11... | collective-permute-start | bytes 983048 | tf_op jit(solution)/shard_map/ppermute | solution.py:565
  52.1 2.2 %copy-start.23 = (bf16[32,2560]{1,0:T(8,128)(2,1)}, bf16[32,2560]{1,0:T(8,128)(2,1)S(1)}, u32[]{:S(2)}) copy-start(bf16[32,2560]{1,0:T(8,128)(2,1)S(1)} %collective-permute-done.17.refs_8_) | copy-start | bytes 491524
  52.1 12.1 %collective-permute-start.18 = (bf16[64,2560]{1,0:T(8,128)(2,1)S(1)}, bf16[64,2560]{1,0:T(8,128)(2,1)S(1)}, u32[]{:S(2)}, u32[]{:S(2)}) collective-permute-start(bf16[64,2560]{1,0:T(8,128)(2,1)S(1)} %collective-permute-done.9.refs_9_), channel_id=1, source_target_pairs={{0,2},{2,6},{6,4},{4,0},{1,3},{3,7},{7,5},{5,1},{8,10},{10,14},{14... | collective-permute-start | bytes 983048 | tf_op jit(solution)/shard_map/ppermute | solution.py:562
  52.3 2.0 %collective-permute-start.8 = (bf16[32,2560]{1,0:T(8,128)(2,1)}, bf16[32,2560]{1,0:T(8,128)(2,1)S(1)}, u32[]{:S(2)}, u32[]{:S(2)}) collective-permute-start(bf16[32,2560]{1,0:T(8,128)(2,1)} %collective-permute-done.7.refs_5_), channel_id=1, source_target_pairs={{0,1},{1,0},{2,3},{3,2},{4,5},{5,4},{6,7},{7,6},{8,9},{9,8},{10,11... | collective-permute-start | bytes 491528 | tf_op jit(solution)/shard_map/ppermute | solution.py:565
  53.1 11.1 %copy-start.19 = (bf16[64,2560]{1,0:T(8,128)(2,1)}, bf16[64,2560]{1,0:T(8,128)(2,1)S(1)}, u32[]{:S(2)}) copy-start(bf16[64,2560]{1,0:T(8,128)(2,1)S(1)} %collective-permute-done.14.refs_10_) | copy-start | bytes 983044
  54.3 0.7 copy-start.24
  55.0 0.7 copy-start.21
  64.2 2.0 %copy-start.20 = (bf16[64,2560]{1,0:T(8,128)(2,1)}, bf16[64,2560]{1,0:T(8,128)(2,1)S(1)}, u32[]{:S(2)}) copy-start(bf16[64,2560]{1,0:T(8,128)(2,1)S(1)} %collective-permute-done.18.refs_13_) | copy-start | bytes 983044
  64.2 1.7 %collective-permute-start.19 = (bf16[64,2560]{1,0:T(8,128)(2,1)S(1)}, bf16[64,2560]{1,0:T(8,128)(2,1)S(1)}, u32[]{:S(2)}, u32[]{:S(2)}) collective-permute-start(bf16[64,2560]{1,0:T(8,128)(2,1)S(1)} %collective-permute-done.18.refs_13_), channel_id=1, source_target_pairs={{0,1},{1,0},{2,3},{3,2},{4,5},{5,4},{6,7},{7,6},{8,9},{9,8},{10,11... | collective-permute-start | bytes 983048 | tf_op jit(solution)/shard_map/ppermute | solution.py:565
  65.9 0.7 copy-start.22
  65.9 17.2 %collective-permute-start.22 = (bf16[1216,640]{1,0:T(8,128)(2,1)}, bf16[1216,640]{1,0:T(8,128)(2,1)S(1)}, u32[]{:S(2)}, u32[]{:S(2)}) collective-permute-start(bf16[1216,640]{1,0:T(8,128)(2,1)} %get-tuple-element.108.refs_7_), channel_id=1, source_target_pairs={{0,1},{1,0},{2,3},{3,2},{4,5},{5,4},{6,7},{7,6},{8,9},{9,8},{10,11... | collective-permute-start | bytes 4669448 | tf_op jit(solution)/shard_map/ppermute | solution.py:565
  77.7 5.4 %copy-start.2 = (bf16[1216,640]{1,0:T(8,128)(2,1)S(1)}, bf16[1216,640]{1,0:T(8,128)(2,1)}, u32[]{:S(2)}) copy-start(bf16[1216,640]{1,0:T(8,128)(2,1)} %get-tuple-element.87.refs_6_.w_own) | copy-start | bytes 4669444
  77.7 1.9 %collective-permute-start.21 = (bf16[128,1216]{1,0:T(8,128)(2,1)}, bf16[128,1216]{1,0:T(8,128)(2,1)S(1)}, u32[]{:S(2)}, u32[]{:S(2)}) collective-permute-start(bf16[128,1216]{1,0:T(8,128)(2,1)} %get-tuple-element.105), channel_id=1, source_target_pairs={{0,1},{1,0},{2,3},{3,2},{4,5},{5,4},{6,7},{7,6},{8,9},{9,8},{10,11... | collective-permute-start | bytes 933896 | tf_op jit(solution)/shard_map/ppermute | solution.py:565
  78.0 5.0 %collective-permute-start.20 = (bf16[384,640]{1,0:T(8,128)(2,1)}, bf16[384,640]{1,0:T(8,128)(2,1)S(1)}, u32[]{:S(2)}, u32[]{:S(2)}) collective-permute-start(bf16[384,640]{1,0:T(8,128)(2,1)} %get-tuple-element.106.own), channel_id=1, source_target_pairs={{0,1},{1,0},{2,3},{3,2},{4,5},{5,4},{6,7},{7,6},{8,9},{9,8},{10,11... | collective-permute-start | bytes 1474568 | tf_op jit(solution)/shard_map/ppermute | solution.py:565
  80.8 8.0 %collective-permute-start.26 = (bf16[64,1216]{1,0:T(8,128)(2,1)S(1)}, bf16[64,1216]{1,0:T(8,128)(2,1)S(1)}, u32[]{:S(2)}, u32[]{:S(2)}) collective-permute-start(bf16[64,1216]{1,0:T(8,128)(2,1)S(1)} %get-tuple-element.124), channel_id=1, source_target_pairs={{0,2},{2,6},{6,4},{4,0},{1,3},{3,7},{7,5},{5,1},{8,10},{10,14},{14... | collective-permute-start | bytes 466952 | tf_op jit(solution)/shard_map/ppermute | solution.py:562
  82.4 9.7 %collective-permute-start.23 = (bf16[64,1216]{1,0:T(8,128)(2,1)S(1)}, bf16[64,1216]{1,0:T(8,128)(2,1)S(1)}, u32[]{:S(2)}, u32[]{:S(2)}) collective-permute-start(bf16[64,1216]{1,0:T(8,128)(2,1)S(1)} %get-tuple-element.125), channel_id=1, source_target_pairs={{0,2},{2,6},{6,4},{4,0},{1,3},{3,7},{7,5},{5,1},{8,10},{10,14},{14... | collective-permute-start | bytes 466952 | tf_op jit(solution)/shard_map/ppermute | solution.py:562
  83.1 1.0 copy-start.6
  85.8 20.7 %copy-start.1 = (f32[128,1216]{1,0:T(8,128)S(1)}, f32[128,1216]{1,0:T(8,128)}, u32[]{:S(2)}) copy-start(f32[128,1216]{1,0:T(8,128)} %get-tuple-element.116.normed) | copy-start | bytes 1867780
  85.8 20.6 %copy-start.5 = (f32[1,1216]{1,0:T(1,128)S(1)}, f32[1,1216]{1,0:T(1,128)}, u32[]{:S(2)}) copy-start(f32[1,1216]{1,0:T(1,128)} %get-tuple-element.115.scale) | copy-start | bytes 14596
  88.8 6.7 %collective-permute-start.27 = (bf16[64,1216]{1,0:T(8,128)(2,1)S(1)}, bf16[64,1216]{1,0:T(8,128)(2,1)S(1)}, u32[]{:S(2)}, u32[]{:S(2)}) collective-permute-start(bf16[64,1216]{1,0:T(8,128)(2,1)S(1)} %add_convert_fusion.2), channel_id=1, source_target_pairs={{0,2},{2,6},{6,4},{4,0},{1,3},{3,7},{7,5},{5,1},{8,10},{10,14},{14... | collective-permute-start | bytes 466952 | tf_op jit(solution)/shard_map/ppermute | solution.py:562
  92.1 16.0 %copy-start.3 = (f32[128,1216]{1,0:T(8,128)S(1)}, f32[128,1216]{1,0:T(8,128)}, u32[]{:S(2)}) copy-start(f32[128,1216]{1,0:T(8,128)} %get-tuple-element.119.base) | copy-start | bytes 1867780
  92.1 16.0 %copy-start.4 = (f32[128,128]{1,0:T(8,128)S(1)}, f32[128,128]{1,0:T(8,128)}, u32[]{:S(2)}) copy-start(f32[128,128]{1,0:T(8,128)} %get-tuple-element.120.inv_std) | copy-start | bytes 196612
  92.1 8.1 %collective-permute-start.24 = (bf16[64,1216]{1,0:T(8,128)(2,1)S(1)}, bf16[64,1216]{1,0:T(8,128)(2,1)S(1)}, u32[]{:S(2)}, u32[]{:S(2)}) collective-permute-start(bf16[64,1216]{1,0:T(8,128)(2,1)S(1)} %add_convert_fusion.4), channel_id=1, source_target_pairs={{0,2},{2,6},{6,4},{4,0},{1,3},{3,7},{7,5},{5,1},{8,10},{10,14},{14... | collective-permute-start | bytes 466952 | tf_op jit(solution)/shard_map/ppermute | solution.py:562
  95.6 7.9 %collective-permute-start.28 = (bf16[64,1216]{1,0:T(8,128)(2,1)S(1)}, bf16[64,1216]{1,0:T(8,128)(2,1)S(1)}, u32[]{:S(2)}, u32[]{:S(2)}) collective-permute-start(bf16[64,1216]{1,0:T(8,128)(2,1)S(1)} %add_convert_fusion.1), channel_id=1, source_target_pairs={{0,2},{2,6},{6,4},{4,0},{1,3},{3,7},{7,5},{5,1},{8,10},{10,14},{14... | collective-permute-start | bytes 466952 | tf_op jit(solution)/shard_map/ppermute | solution.py:562
  100.2 6.3 %collective-permute-start.25 = (bf16[64,1216]{1,0:T(8,128)(2,1)S(1)}, bf16[64,1216]{1,0:T(8,128)(2,1)S(1)}, u32[]{:S(2)}, u32[]{:S(2)}) collective-permute-start(bf16[64,1216]{1,0:T(8,128)(2,1)S(1)} %add_convert_fusion.3), channel_id=1, source_target_pairs={{0,2},{2,6},{6,4},{4,0},{1,3},{3,7},{7,5},{5,1},{8,10},{10,14},{14... | collective-permute-start | bytes 466952 | tf_op jit(solution)/shard_map/ppermute | solution.py:562
  106.7 1.3 %collective-permute-start.29 = (f32[128,128]{1,0:T(8,128)S(1)}, f32[128,128]{1,0:T(8,128)S(1)}, u32[]{:S(2)}, u32[]{:S(2)}) collective-permute-start(f32[128,128]{1,0:T(8,128)S(1)} %get-tuple-element.118.sums), channel_id=1, source_target_pairs={{0,1},{1,0},{2,3},{3,2},{4,5},{5,4},{6,7},{7,6},{8,9},{9,8},{10,11... | collective-permute-start | bytes 196616 | tf_op jit(solution)/shard_map/ppermute | solution.py:565
